TPU v7x, 32 devices: a whole 2x2x4 slice. The times are simulated.
32 devices in a mesh: pipe: 4 (over z), expert: 8 (over y, x, core).
Axes of the slice: x: 2, y: 2, z: 4, core: 2. Of those that a mesh axis runs over, the one named last changes fastest.
Arguments:
- inputs: bfloat16 [4, 1024, 4096], P('pipe', 'expert'), may hold values from -6 to 6
- upstream: bfloat16 [4, 1024, 4096], P('pipe', 'expert'), may hold values from -24 to 24
- route: int32 [4, 1024, 8], P('pipe', 'expert'), may hold values from 0 to 127, as said below
- prob: float32 [4, 1024, 8], P('pipe', 'expert'), may hold values from 0.05 to 0.4
- gate_up: bfloat16 [4, 8, 4096, 384], P('pipe', 'expert'), may hold values from -0.09375 to 0.09375
- down: bfloat16 [4, 8, 192, 4096], P('pipe', 'expert'), may hold values from -0.15625 to 0.15625
Outputs:
- grad_input: bfloat16 [4, 1024, 4096], P('pipe', 'expert')
- grad_gate_up: bfloat16 [4, 8, 4096, 384], P('pipe', 'expert')
- grad_down: bfloat16 [4, 8, 192, 4096], P('pipe', 'expert')
Inputs may be any that keep to these rules, and one draw needn't show every extreme that they name: `route`: each token names 8 different experts and at most one expert below 1. In each aligned block of 128 tokens of a section every expert below 1 is named by 1 to 8 tokens; one such expert, the same for all blocks, is named by exactly 8 tokens of every block.
All inputs are finite; a program needn't handle non-finite values.
Results may differ from a plain program's by a relative error of at most 0.014.
Values may be sent and summed in bfloat16 or wider, within the bound.
A program may use at most 128 MiB of HBM per device.

v0:
```python
import jax
import jax.numpy as jnp
from jax import lax
from jax.sharding import PartitionSpec as P

SPLIT = 8
CAP = 8


def shifted(block, axis, distance):
    devices = range(lax.axis_size(axis))
    route = [((i - distance) % len(devices), i) for i in devices]
    return lax.ppermute(block, axis, route)


def shards(inputs, upstream, route, prob, gate_up, down):
    arrived = shifted(upstream, "pipe", -1)[0]
    layer_in = inputs[0]
    slot_route = route[0]
    slot_prob = prob[0]
    groups = lax.axis_size("expert")
    flight = groups // SPLIT
    width = layer_in.shape[1]
    experts_here = jnp.arange(flight, dtype=jnp.int32)
    hits = slot_route[:, :, None] == experts_here[None, None, :]
    weight = jnp.sum(jnp.where(hits, slot_prob[:, :, None], jnp.float32(0.0)), axis=1)
    member = jnp.any(hits, axis=1).astype(jnp.int32)
    rank = jnp.cumsum(member, axis=0) - member
    slot_ids = jnp.arange(CAP, dtype=jnp.int32)
    select = (member.T[:, None, :] == 1) & (rank.T[:, None, :] == slot_ids[None, :, None])
    picker = select.astype(jnp.bfloat16)
    rows_x = jnp.einsum("ect,td->ecd", picker, layer_in, preferred_element_type=jnp.float32).astype(
        jnp.bfloat16
    )
    rows_g = jnp.einsum("ect,td->ecd", picker, arrived, preferred_element_type=jnp.float32)
    slot_weight = jnp.sum(jnp.where(select, weight.T[:, None, :], jnp.float32(0.0)), axis=2)
    rows_e = (rows_g * slot_weight[:, :, None]).astype(jnp.bfloat16)
    mine = lax.axis_index("expert") // SPLIT
    all_x, all_e = (
        lax.all_gather(rows_x[None], "expert", axis=0, tiled=True),
        lax.all_gather(rows_e[None], "expert", axis=0, tiled=True),
    )
    got_x = lax.dynamic_index_in_dim(all_x, mine, axis=1, keepdims=False)
    got_e = lax.dynamic_index_in_dim(all_e, mine, axis=1, keepdims=False)
    flat_x = got_x.reshape(-1, width)
    flat_e = got_e.reshape(-1, width)
    w_both = gate_up[0, 0]
    w_down = down[0, 0]
    hidden_cols = w_down.shape[0]
    both = jnp.dot(flat_x, w_both, preferred_element_type=jnp.float32)
    pre_gate = both[:, :hidden_cols]
    pre_up = both[:, hidden_cols:]
    sigma = jax.nn.sigmoid(pre_gate)
    silu_val = pre_gate * sigma
    hidden = (silu_val * pre_up).astype(jnp.bfloat16)
    grad_hidden = lax.dot_general(
        flat_e, w_down, (((1,), (1,)), ((), ())), preferred_element_type=jnp.float32
    )
    grad_a = (grad_hidden * pre_up * sigma * (1.0 + pre_gate * (1.0 - sigma))).astype(jnp.bfloat16)
    grad_u = (grad_hidden * silu_val).astype(jnp.bfloat16)
    grad_both = jnp.concatenate([grad_a, grad_u], axis=1)
    grad_down = lax.dot_general(
        hidden, flat_e, (((0,), (0,)), ((), ())), preferred_element_type=jnp.float32
    ).astype(jnp.bfloat16)
    grad_gu = lax.dot_general(
        flat_x, grad_both, (((0,), (0,)), ((), ())), preferred_element_type=jnp.float32
    ).astype(jnp.bfloat16)
    partial_value = lax.dot_general(
        grad_both, w_both, (((1,), (1,)), ((), ())), preferred_element_type=jnp.float32
    ).astype(jnp.bfloat16)
    returned = lax.all_to_all(
        partial_value.reshape(groups, CAP, width), "expert", split_axis=0, concat_axis=0, tiled=True
    )
    summed = jnp.sum(returned.astype(jnp.float32).reshape(flight, SPLIT, CAP, width), axis=1)
    grad_x = jnp.einsum(
        "ect,ecd->td", select.astype(jnp.float32), summed, precision=lax.Precision.HIGHEST
    )
    return (grad_x.astype(jnp.bfloat16)[None], grad_gu[None, None], grad_down[None, None])


def solution(mesh):
    placed = (
        P("pipe", "expert", None),
        P("pipe", "expert", None),
        P("pipe", "expert", None),
        P("pipe", "expert", None),
        P("pipe", "expert", None, None),
        P("pipe", "expert", None, None),
    )
    return jax.shard_map(
        shards,
        mesh=mesh,
        in_specs=placed,
        out_specs=(
            P("pipe", "expert", None),
            P("pipe", "expert", None, None),
            P("pipe", "expert", None, None),
        ),
        check_vma=False,
    )
```

profile of v0, /device:TPU:0, one launch (start us, length us, event | category | flops | bytes accessed | tf_op | source)
XLA Modules:
  0.0 60.2 jit_solution(17145834383001678684)
XLA Ops:
  0.6 0.0 copy-start
  0.6 5.1 %collective-permute-start = (bf16[1,128,4096]{2,1,0:T(8,128)(2,1)}, bf16[1,128,4096]{2,1,0:T(8,128)(2,1)}, u32[]{:S(2)}, u32[]{:S(2)}) collective-permute-start(bf16[1,128,4096]{2,1,0:T(8,128)(2,1)} %param.7), channel_id=1, source_target_pairs={{8,0},{16,8},{24,16},{0,24},{9,1},{17,9},{25,17},{1,25},{10,2},{18... | collective-permute-start | bytes 3145736 | tf_op jit(solution)/shard_map/ppermute | solution.py:13
  5.7 0.7 %fusion.28 = (pred[128]{0:T(512)(128)(4,1)S(1)}, pred[1,128,8]{1,2,0:T(8,128)(4,1)S(1)}) fusion(s32[1,128,8]{1,2,0:T(8,128)} %param.8), kind=kLoop, calls=%fused_computation.44 | loop fusion | flops 1920 | bytes 5248 | tf_op jit(solution)/shard_map/reduce_or | solution.py:27
  6.5 0.7 %select_reduce_fusion.1 = f32[128]{0:T(128)S(1)} fusion(pred[1,128,8]{1,2,0:T(8,128)(4,1)S(1)} %get-tuple-element.4, f32[1,128,8]{1,2,0:T(8,128)} %param.9), kind=kLoop, calls=%fused_computation.26 | loop fusion | flops 1920 | bytes 5632 | tf_op jit(solution)/shard_map/reduce_sum | solution.py:26
  7.2 0.1 copy.11
  7.3 0.2 reduce-window.7
  7.5 0.1 reduce.7
  7.6 0.1 select_reduce_fusion
  7.7 1.5 %convolution_convert_fusion.4 = bf16[8,4096]{1,0:T(8,128)(2,1)S(1)} fusion(bf16[1,128,4096]{2,1,0:T(8,128)(2,1)} %param.6, s32[128]{0:T(128)S(1)} %convert_subtract_fusion, pred[128]{0:T(512)(128)(4,1)S(1)} %get-tuple-element.7), kind=kOutput, calls=%fused_computation.10 | convolution fusion | flops 8423424 | bytes 1114752 | tf_op jit(solution)/shard_map/ect,td->ecd/dot_general | solution.py:32
  9.2 0.0 copy-start.3
  9.2 10.0 %all-gather.1 = bf16[64,4096]{1,0:T(8,128)(2,1)S(1)} all-gather(bf16[8,4096]{1,0:T(8,128)(2,1)S(1)} %convolution_convert_fusion.4), channel_id=3, replica_groups=mesh['pipe'=4,'expert'=8] {'expert'}, dimensions={0}, use_global_device_ids=true | all-gather | bytes 589824 | tf_op jit(solution)/shard_map/all_gather | solution.py:40
  19.2 0.0 copy-start.1
  19.2 0.8 %copy-done.1 = bf16[64,4096]{1,0:T(8,128)(2,1)} copy-done((bf16[64,4096]{1,0:T(8,128)(2,1)}, bf16[64,4096]{1,0:T(8,128)(2,1)S(1)}, u32[]{:S(2)}) %copy-start.1) | copy-done | bytes 524312
  20.0 0.0 copy-done
  20.0 0.6 fusion.6
  20.6 7.9 %collective-permute-done = bf16[1,128,4096]{2,1,0:T(8,128)(2,1)} collective-permute-done((bf16[1,128,4096]{2,1,0:T(8,128)(2,1)}, bf16[1,128,4096]{2,1,0:T(8,128)(2,1)}, u32[]{:S(2)}, u32[]{:S(2)}) %collective-permute-start) | collective-permute-done | bytes 1048608 | tf_op jit(solution)/shard_map/ppermute | solution.py:13
  28.5 1.5 %fusion.4 = bf16[8,4096]{1,0:T(8,128)(2,1)S(1)} fusion(bf16[1,128,4096]{2,1,0:T(8,128)(2,1)} %collective-permute-done, f32[8]{0:T(128)S(1)} %select_reduce_fusion, s32[128]{0:T(128)S(1)} %convert_subtract_fusion, pred[128]{0:T(512)(128)(4,1)S(1)} %get-tuple-element.7), kind=kOutput, calls=%fused_computation.9 | convolution fusion | flops 8456192 | bytes 1114784 | tf_op jit(solution)/shard_map/ect,td->ecd/dot_general | solution.py:35
  30.0 9.9 %all-gather = bf16[64,4096]{1,0:T(8,128)(2,1)S(1)} all-gather(bf16[8,4096]{1,0:T(8,128)(2,1)S(1)} %fusion.4), channel_id=2, replica_groups=mesh['pipe'=4,'expert'=8] {'expert'}, dimensions={0}, use_global_device_ids=true | all-gather | bytes 589824 | tf_op jit(solution)/shard_map/all_gather | solution.py:41
  39.8 0.0 copy-start.2
  39.8 0.8 %copy-done.2 = bf16[64,4096]{1,0:T(8,128)(2,1)} copy-done((bf16[64,4096]{1,0:T(8,128)(2,1)}, bf16[64,4096]{1,0:T(8,128)(2,1)S(1)}, u32[]{:S(2)}) %copy-start.2) | copy-done | bytes 524312
  40.6 0.0 copy-done.3
  40.6 0.6 %multiply_convert_fusion.2 = (bf16[64,192]{1,0:T(8,128)(2,1)S(1)}, bf16[64,192]{1,0:T(8,128)(2,1)S(1)}) fusion(f32[64,384]{1,0:T(8,128)S(1)} %fusion.6, bf16[64,4096]{1,0:T(8,128)(2,1)S(1)} %all-gather, bf16[1,1,192,4096]{3,2,1,0:T(8,128)(2,1)S(1)} %copy-done.3), kind=kOutput, calls=%fused_computation.21 | convolution fusion | flops 100823040 | bytes 2244608 | tf_op jit(solution)/shard_map/dot_general | solution.py:56
  41.2 1.9 %fusion.3 = bf16[8,8,4096]{2,1,0:T(8,128)(2,1)} fusion(bf16[1,1,4096,384]{3,2,1,0:T(8,128)(2,1)S(1)} %copy-done, bf16[64,192]{1,0:T(8,128)(2,1)S(1)} %get-tuple-element.6, bf16[64,192]{1,0:T(8,128)(2,1)S(1)} %get-tuple-element.5), kind=kOutput, calls=%fused_computation.7 | convolution fusion | flops 201687040 | bytes 3719168 | tf_op jit(solution)/shard_map/dot_general | solution.py:68
  43.2 4.1 %all-to-all-start = ((bf16[8,8,4096]{2,1,0:T(8,128)(2,1)}), bf16[8,8,4096]{2,1,0:T(8,128)(2,1)}, u32[]{:S(2)}, u32[]{:S(2)}) async-start(bf16[8,8,4096]{2,1,0:T(8,128)(2,1)} %fusion.3), calls=%async_computation | async-start | bytes 1048576 | tf_op jit(solution)/shard_map/all_to_all | solution.py:71
  47.3 2.9 %fusion.1 = bf16[1,1,192,4096]{3,2,1,0:T(8,128)(2,1)} fusion(bf16[64,4096]{1,0:T(8,128)(2,1)} %copy-done.2, f32[64,384]{1,0:T(8,128)S(1)} %fusion.6), kind=kOutput, calls=%fused_computation.4 | convolution fusion | flops 101523456 | bytes 2228224 | tf_op jit(solution)/shard_map/dot_general | solution.py:62
  50.2 3.8 %fusion = bf16[1,1,4096,384]{3,2,1,0:T(8,128)(2,1)} fusion(bf16[64,4096]{1,0:T(8,128)(2,1)} %copy-done.1, bf16[64,192]{1,0:T(8,128)(2,1)S(1)} %get-tuple-element.6, bf16[64,192]{1,0:T(8,128)(2,1)S(1)} %get-tuple-element.5), kind=kOutput, calls=%fused_computation.1 | convolution fusion | flops 202997760 | bytes 3719168 | tf_op jit(solution)/shard_map/dot_general | solution.py:65
  53.9 3.1 %all-to-all-done = bf16[8,8,4096]{2,1,0:T(8,128)(2,1)} async-done(((bf16[8,8,4096]{2,1,0:T(8,128)(2,1)}), bf16[8,8,4096]{2,1,0:T(8,128)(2,1)}, u32[]{:S(2)}, u32[]{:S(2)}) %all-to-all-start) | async-done | bytes 524320 | tf_op jit(solution)/shard_map/all_to_all | solution.py:71
  57.1 1.1 %convert_reduce_fusion = f32[8,4096]{1,0:T(8,128)S(1)} fusion(bf16[8,8,4096]{2,1,0:T(8,128)(2,1)} %all-to-all-done), kind=kLoop, calls=%fused_computation.18 | loop fusion | flops 491520 | bytes 655360 | tf_op jit(solution)/shard_map/reduce_sum | solution.py:74
  58.2 2.0 %fusion.2 = bf16[1,128,4096]{2,1,0:T(8,128)(2,1)} fusion(f32[8,4096]{1,0:T(8,128)S(1)} %convert_reduce_fusion, s32[128]{0:T(128)S(1)} %convert_subtract_fusion, pred[128]{0:T(512)(128)(4,1)S(1)} %get-tuple-element.7), kind=kOutput, calls=%fused_computation.5 | convolution fusion | flops 50857984 | bytes 1180288 | tf_op jit(solution)/shard_map/ect,ecd->td/dot_general | solution.py:75
  (2 shorter events, 0.0 us)
Async XLA Ops:
  0.6 19.3 %copy-start = (bf16[1,1,4096,384]{3,2,1,0:T(8,128)(2,1)S(1)}, bf16[1,1,4096,384]{3,2,1,0:T(8,128)(2,1)}, u32[]{:S(2)}) copy-start(bf16[1,1,4096,384]{3,2,1,0:T(8,128)(2,1)} %param.10) | copy-start | bytes 9437188
  0.6 27.8 %collective-permute-start = (bf16[1,128,4096]{2,1,0:T(8,128)(2,1)}, bf16[1,128,4096]{2,1,0:T(8,128)(2,1)}, u32[]{:S(2)}, u32[]{:S(2)}) collective-permute-start(bf16[1,128,4096]{2,1,0:T(8,128)(2,1)} %param.7), channel_id=1, source_target_pairs={{8,0},{16,8},{24,16},{0,24},{9,1},{17,9},{25,17},{1,25},{10,2},{18... | collective-permute-start | bytes 3145736 | tf_op jit(solution)/shard_map/ppermute | solution.py:13
  9.2 31.4 %copy-start.3 = (bf16[1,1,192,4096]{3,2,1,0:T(8,128)(2,1)S(1)}, bf16[1,1,192,4096]{3,2,1,0:T(8,128)(2,1)}, u32[]{:S(2)}) copy-start(bf16[1,1,192,4096]{3,2,1,0:T(8,128)(2,1)} %param.11) | copy-start | bytes 4718596
  19.2 0.8 %copy-start.1 = (bf16[64,4096]{1,0:T(8,128)(2,1)}, bf16[64,4096]{1,0:T(8,128)(2,1)S(1)}, u32[]{:S(2)}) copy-start(bf16[64,4096]{1,0:T(8,128)(2,1)S(1)} %all-gather.1) | copy-start | bytes 1572868
  39.8 0.8 %copy-start.2 = (bf16[64,4096]{1,0:T(8,128)(2,1)}, bf16[64,4096]{1,0:T(8,128)(2,1)S(1)}, u32[]{:S(2)}) copy-start(bf16[64,4096]{1,0:T(8,128)(2,1)S(1)} %all-gather) | copy-start | bytes 1572868
  43.2 13.9 %all-to-all-start = ((bf16[8,8,4096]{2,1,0:T(8,128)(2,1)}), bf16[8,8,4096]{2,1,0:T(8,128)(2,1)}, u32[]{:S(2)}, u32[]{:S(2)}) async-start(bf16[8,8,4096]{2,1,0:T(8,128)(2,1)} %fusion.3), calls=%async_computation | async-start | bytes 1048576 | tf_op jit(solution)/shard_map/all_to_all | solution.py:71
where the time goes:
time: 60.7 us; the launch traced here: 60.2 us
  blocking collectives  19.8 us (33%)
  matrix products  14.7 us (24%)
  waiting for transfers between devices  11.1 us (18%)
  starting transfers between devices  9.25 us (15%)
  other arithmetic  2.94 us (5%)
  local copies, waits for them, and re-layouts  1.73 us (3%)
  between operations  0.68 us (1%)
    all_gather x1, blocking collectives, shards(): lax.all_gather(rows_x[None], 'expert', axis=0, tiled=True)  9.99 us
    all_gather x1, blocking collectives, shards(): lax.all_gather(rows_e[None], 'expert', axis=0, tiled=True)  9.85 us
    ppermute x1, waiting for transfers between devices, shifted(): return lax.ppermute(block, axis, route)  7.91 us
    ppermute x1, starting transfers between devices, shifted(): return lax.ppermute(block, axis, route)  5.1 us
    all_to_all x1, starting transfers between devices, shards(): lax.all_to_all(partial_value.reshape(groups, CAP, width), 'expert', split...  4.14 us
    dot_general x1, matrix products, shards(): lax.dot_general(flat_x, grad_both, (((0,), (0,)), ((), ())), preferred_el...  3.75 us
    all_to_all x1, waiting for transfers between devices, shards(): lax.all_to_all(partial_value.reshape(groups, CAP, width), 'expert', split...  3.14 us
    dot_general x1, matrix products, shards(): lax.dot_general(hidden, flat_e, (((0,), (0,)), ((), ())), preferred_eleme...  2.86 us
  transfers between devices with their start and end apart: 2, of which 2 were waited for; matrix products, arithmetic and copies ran while one was open for 18% of the time, Pallas kernels for 0%

commit v1 on v0

v1 whole, which is shorter than its diff:
```python
import functools

import jax
import jax.numpy as jnp
from jax import lax
from jax.experimental import pallas as pl
from jax.experimental.pallas import tpu as pltpu
from jax.sharding import PartitionSpec as P

SPLIT = 8
CAP = 8
CORES = 2
E_PARTS = 2
OUT_PARTS = 4
MESH = pl.DeviceIdType.MESH
F32 = jnp.float32
BF16 = jnp.bfloat16


def dot(a, b, dims):
    return lax.dot_general(a, b, (dims, ((), ())), preferred_element_type=F32)


def remote(src, dst, send, recv, target):
    return pltpu.make_async_remote_copy(
        src_ref=src, dst_ref=dst, send_sem=send, recv_sem=recv, device_id=target, device_id_type=MESH
    )


def exchange(
    sections, chips, flight,
    x_hbm, u_hbm, route_hbm, prob_hbm, gu_hbm, dn_hbm,
    ggu, gdn, sums, sel_out,
    x_v, u_v, route_v, prob_v, w_gu, w_dn,
    s_out, s_in, xb, xg, eb, er, eg, pair_in, keep, ro, rin,
    local, s_sem, x_send, x_recv, xf_send, xf_recv,
    z_send, z_recv, e_send, e_recv, ef_send, ef_recv,
    p_send, p_recv, r_send, r_recv,
):
    section = lax.axis_index("pipe")
    me = lax.axis_index("expert")
    chip, core = me // CORES, me % CORES
    mine = me // SPLIT
    sibling = {"expert": me + 1 - 2 * core}
    ahead = {"pipe": (section + 1) % sections}
    behind = {"pipe": (section + sections - 1) % sections}
    width = x_v.shape[1]
    tokens = x_v.shape[0]
    hid = w_dn.shape[0]

    def chip_at(d):
        return (chip + d) % chips

    def chip_from(d):
        return (chip + chips - d) % chips

    def peer(d):
        return {"expert": chip_at(d) * CORES + core}

    loads = [
        pltpu.make_async_copy(src, dst, local.at[k])
        for k, (src, dst) in enumerate(
            (
                (route_hbm.at[0], route_v),
                (prob_hbm.at[0], prob_v),
                (x_hbm.at[0], x_v),
                (u_hbm.at[0], u_v),
                (gu_hbm.at[0, 0], w_gu),
                (dn_hbm.at[0, 0], w_dn),
            )
        )
    ]
    for load in loads:
        load.start()
    barrier = pltpu.get_barrier_semaphore()
    for target in [sibling, ahead, behind] + [peer(d) for d in range(1, chips)]:
        pl.semaphore_signal(barrier, inc=1, device_id=target, device_id_type=MESH)
    loads[0].wait()
    loads[1].wait()
    before = (
        lax.broadcasted_iota(jnp.int32, (tokens, tokens), 0)
        < lax.broadcasted_iota(jnp.int32, (tokens, tokens), 1)
    ).astype(F32).astype(BF16)
    slots = lax.broadcasted_iota(jnp.int32, (CAP, tokens), 0).astype(F32)
    picks = []
    for e in range(flight):
        hit = route_v[...] == e
        member = jnp.max(jnp.where(hit, 1.0, 0.0), axis=0, keepdims=True)
        weight = jnp.sum(jnp.where(hit, prob_v[...], 0.0), axis=0, keepdims=True)
        member = jnp.broadcast_to(member, (CAP, tokens))
        rank = dot(member.astype(BF16), before, ((1,), (0,)))
        chosen = jnp.where((member > 0.0) & (rank == slots), 1.0, 0.0)
        sel_out[e] = chosen
        s_out[e] = chosen * weight
        picks.append(chosen.astype(BF16))
    pl.semaphore_wait(barrier, chips + 2)

    send_s = remote(s_out, s_in, s_sem.at[0], s_sem.at[1], ahead)
    send_s.start()
    sends = [send_s]

    loads[2].wait()
    for e in range(flight):
        xb[e] = dot(picks[e], x_v[...], ((1,), (0,))).astype(BF16)
    for d in range(1, chips):
        copy = remote(
            xb.at[chip_at(d) * CORES // SPLIT], xg.at[core, chip], x_send.at[d], x_recv.at[d], peer(d)
        )
        copy.start()
        sends.append(copy)
    copy = remote(xb.at[mine], xg.at[core, chip], xf_send.at[0], xf_recv.at[0], sibling)
    copy.start()
    sends.append(copy)
    xg[core, chip] = xb[mine]

    loads[3].wait()
    send_s.wait_recv()
    e_cols = width // E_PARTS
    scales, gpicks = [], []
    for e in range(flight):
        weights = s_in[e]
        scales.append(jnp.sum(weights, axis=1, keepdims=True))
        gpicks.append(jnp.where(weights > 0.0, 1.0, 0.0).astype(BF16))
    z_copies = []
    for k in range(E_PARTS):
        cols = pl.ds(k * e_cols, e_cols)
        for e in range(flight):
            eb[e, :, cols] = (dot(gpicks[e], u_v[:, cols], ((1,), (0,))) * scales[e]).astype(BF16)
        copy = remote(eb.at[:, :, cols], er.at[:, :, cols], z_send.at[k], z_recv.at[k], behind)
        copy.start()
        z_copies.append(copy)
    sends.extend(z_copies)

    def relay(buf, d, cols, recv, f_send, f_recv):
        slot = buf.at[core, chip_from(d), :, cols]
        remote(slot, slot, f_send, recv, sibling).wait_recv()
        copy = remote(slot, slot, f_send, f_recv, sibling)
        copy.start()
        sends.append(copy)

    def from_sibling(buf, d, cols, f_send, f_recv):
        slot = buf.at[1 - core, chip_from(d), :, cols]
        remote(slot, slot, f_send, f_recv, sibling).wait_recv()

    every = pl.ds(0, width)
    for d in range(1, chips):
        relay(xg, d, every, x_recv.at[d], xf_send.at[d], xf_recv.at[d])
    for k in range(E_PARTS):
        cols = pl.ds(k * e_cols, e_cols)
        z_copies[k].wait_recv()
        for d in range(1, chips):
            copy = remote(
                er.at[chip_at(d) * CORES // SPLIT, :, cols],
                eg.at[core, chip, :, cols],
                e_send.at[k, d],
                e_recv.at[k, d],
                peer(d),
            )
            copy.start()
            sends.append(copy)
        copy = remote(
            er.at[mine, :, cols], eg.at[core, chip, :, cols], ef_send.at[k, 0], ef_recv.at[k, 0], sibling
        )
        copy.start()
        sends.append(copy)
        eg[core, chip, :, cols] = er[mine, :, cols]
    for d in range(chips):
        from_sibling(xg, d, every, xf_send.at[d], xf_recv.at[d])
    rows = CORES * chips * CAP
    loads[4].wait()
    both = dot(xg[...].reshape(rows, width), w_gu[...], ((1,), (0,)))
    pre_gate = both[:, :hid]
    pre_up = both[:, hid:]
    sigma = jax.nn.sigmoid(pre_gate)
    silu_val = pre_gate * sigma
    hidden = (silu_val * pre_up).astype(BF16)
    slope = pre_up * sigma * (1.0 + pre_gate * (1.0 - sigma))

    loads[5].wait()
    grad_hidden = None
    for k in range(E_PARTS):
        cols = pl.ds(k * e_cols, e_cols)
        for d in range(1, chips):
            relay(eg, d, cols, e_recv.at[k, d], ef_send.at[k, d], ef_recv.at[k, d])
    for k in range(E_PARTS):
        cols = pl.ds(k * e_cols, e_cols)
        for d in range(chips):
            from_sibling(eg, d, cols, ef_send.at[k, d], ef_recv.at[k, d])
        term = dot(eg[:, :, :, cols].reshape(rows, e_cols), w_dn[:, cols], ((1,), (1,)))
        grad_hidden = term if grad_hidden is None else grad_hidden + term
    grad_both = jnp.concatenate([grad_hidden * slope, grad_hidden * silu_val], axis=1).astype(BF16)

    o_cols = width // OUT_PARTS
    pair = []
    for k in range(OUT_PARTS):
        cols = pl.ds(k * o_cols, o_cols)
        part = dot(grad_both, w_gu[cols, :], ((1,), (1,))).astype(BF16)
        keep[:, :, :, cols] = part.reshape(CORES, chips, CAP, o_cols)
        copy = remote(
            keep.at[1 - core, :, :, cols], pair_in.at[:, :, cols], p_send.at[k], p_recv.at[k], sibling
        )
        copy.start()
        pair.append(copy)
    sends.extend(pair)
    for k in range(OUT_PARTS):
        cols = pl.ds(k * o_cols, o_cols)
        pair[k].wait_recv()
        ro[:, :, cols] = (keep[core, :, :, cols].astype(F32) + pair_in[:, :, cols].astype(F32)).astype(BF16)
        for d in range(1, chips):
            copy = remote(
                ro.at[chip_at(d), :, cols], rin.at[chip, :, cols], r_send.at[k, d], r_recv.at[k, d], peer(d)
            )
            copy.start()
            sends.append(copy)
        rin[chip, :, cols] = ro[chip, :, cols]

    for k in range(OUT_PARTS):
        cols = pl.ds(k * o_cols, o_cols)
        x_part = xg[:, :, :, cols].reshape(rows, o_cols)
        ggu[cols, :] = dot(x_part, grad_both, ((0,), (0,))).astype(BF16)
        e_part = eg[:, :, :, cols].reshape(rows, o_cols)
        gdn[:, cols] = dot(hidden, e_part, ((0,), (0,))).astype(BF16)

    per = chips // flight
    for k in range(OUT_PARTS):
        cols = pl.ds(k * o_cols, o_cols)
        for d in range(1, chips):
            slot = rin.at[chip_from(d), :, cols]
            remote(slot, slot, r_send.at[k, d], r_recv.at[k, d], peer(d)).wait_recv()
        for e in range(flight):
            total = rin[e * per, :, cols].astype(F32)
            for q in range(1, per):
                total = total + rin[e * per + q, :, cols].astype(F32)
            sums[e, :, cols] = total.astype(BF16)
    for copy in sends:
        copy.wait_send()


def finish(flight, ggu, gdn, sums, sel, gi_hbm, gu_hbm, dn_hbm, gi_v, sems):
    copies = [
        pltpu.make_async_copy(ggu, gu_hbm.at[0, 0], sems.at[0]),
        pltpu.make_async_copy(gdn, dn_hbm.at[0, 0], sems.at[1]),
    ]
    for copy in copies:
        copy.start()
    total = None
    for e in range(flight):
        term = dot(sel[e].astype(BF16), sums[e], ((0,), (0,)))
        total = term if total is None else total + term
    gi_v[...] = total.astype(BF16)
    last = pltpu.make_async_copy(gi_v, gi_hbm.at[0], sems.at[2])
    last.start()
    for copy in copies + [last]:
        copy.wait()


def shards(inputs, upstream, route, prob, gate_up, down):
    sections = lax.axis_size("pipe")
    groups = lax.axis_size("expert")
    chips = groups // CORES
    flight = groups // SPLIT
    _, tokens, width = inputs.shape
    slots = route.shape[2]
    both_cols = gate_up.shape[3]
    hid = down.shape[2]
    dma = pltpu.SemaphoreType.DMA
    anywhere = pl.BlockSpec(memory_space=pl.ANY)
    vmem = pl.BlockSpec(memory_space=pltpu.VMEM)
    kept = pltpu.VMEM
    ggu, gdn, sums, sel = pl.pallas_call(
        functools.partial(exchange, sections, chips, flight),
        out_shape=(
            kept((width, both_cols), BF16),
            kept((hid, width), BF16),
            kept((flight, CAP, width), BF16),
            kept((flight, CAP, tokens), F32),
        ),
        in_specs=[anywhere] * 6,
        out_specs=(vmem,) * 4,
        scratch_shapes=[
            pltpu.VMEM((tokens, width), BF16),
            pltpu.VMEM((tokens, width), BF16),
            pltpu.VMEM((slots, tokens), jnp.int32),
            pltpu.VMEM((slots, tokens), F32),
            pltpu.VMEM((width, both_cols), BF16),
            pltpu.VMEM((hid, width), BF16),
            pltpu.VMEM((flight, CAP, tokens), F32),
            pltpu.VMEM((flight, CAP, tokens), F32),
            pltpu.VMEM((flight, CAP, width), BF16),
            pltpu.VMEM((CORES, chips, CAP, width), BF16),
            pltpu.VMEM((flight, CAP, width), BF16),
            pltpu.VMEM((flight, CAP, width), BF16),
            pltpu.VMEM((CORES, chips, CAP, width), BF16),
            pltpu.VMEM((chips, CAP, width), BF16),
            pltpu.VMEM((CORES, chips, CAP, width), BF16),
            pltpu.VMEM((chips, CAP, width), BF16),
            pltpu.VMEM((chips, CAP, width), BF16),
            dma((6,)),
            dma((2,)),
            dma((chips,)),
            dma((chips,)),
            dma((chips,)),
            dma((chips,)),
            dma((E_PARTS,)),
            dma((E_PARTS,)),
            dma((E_PARTS, chips)),
            dma((E_PARTS, chips)),
            dma((E_PARTS, chips)),
            dma((E_PARTS, chips)),
            dma((OUT_PARTS,)),
            dma((OUT_PARTS,)),
            dma((OUT_PARTS, chips)),
            dma((OUT_PARTS, chips)),
        ],
        compiler_params=pltpu.CompilerParams(
            collective_id=0, has_side_effects=True, vmem_limit_bytes=40 * 2**20
        ),
    )(inputs, upstream, jnp.swapaxes(route, 1, 2), jnp.swapaxes(prob, 1, 2), gate_up, down)
    return pl.pallas_call(
        functools.partial(finish, flight),
        out_shape=(
            jax.ShapeDtypeStruct(inputs.shape, BF16),
            jax.ShapeDtypeStruct(gate_up.shape, BF16),
            jax.ShapeDtypeStruct(down.shape, BF16),
        ),
        in_specs=[vmem] * 4,
        out_specs=(anywhere,) * 3,
        scratch_shapes=[pltpu.VMEM((tokens, width), BF16), dma((3,))],
        compiler_params=pltpu.CompilerParams(vmem_limit_bytes=16 * 2**20),
    )(ggu, gdn, sums, sel)


def solution(mesh):
    placed = (
        P("pipe", "expert", None),
        P("pipe", "expert", None),
        P("pipe", "expert", None),
        P("pipe", "expert", None),
        P("pipe", "expert", None, None),
        P("pipe", "expert", None, None),
    )
    return jax.shard_map(
        shards,
        mesh=mesh,
        in_specs=placed,
        out_specs=(
            P("pipe", "expert", None),
            P("pipe", "expert", None, None),
            P("pipe", "expert", None, None),
        ),
        check_vma=False,
    )
```

time: 60.7 us -> 36.3 us (0.60)
  Pallas kernels: 0 us -> 28.3 us
  blocking collectives: 19.8 us -> 0 us
  matrix products: 14.7 us -> 0 us
  waiting for transfers between devices: 11.1 us -> 0 us
  starting transfers between devices: 9.25 us -> 0 us
  local copies, waits for them, and re-layouts: 1.73 us -> 7.11 us
  other arithmetic: 2.94 us -> 0 us
    pallas_call x0 -> x2, Pallas kernels: none -> 28.3 us  [the longest x1 25.7 us: shards(): pl.pallas_call(functools.partial(exchange, sections, chips, flight), out_...]
    all_gather x2 -> x0, blocking collectives: 19.8 us -> none  [the longest x1 9.99 us: shards(): lax.all_gather(rows_x[None], 'expert', axis=0, tiled=True)]
    dot_general x8 -> x0, matrix products: 14.7 us -> none  [the longest x1 3.75 us: shards(): lax.dot_general(flat_x, grad_both, (((0,), (0,)), ((), ())), preferred_el...]
    ppermute x1 -> x0, waiting for transfers between devices: 7.91 us -> none  [shifted(): return lax.ppermute(block, axis, route)]
    unnamed x8 -> x12, local copies, waits for them, and re-layouts: 1.62 us -> 7.11 us
    ppermute x1 -> x0, starting transfers between devices: 5.1 us -> none  [shifted(): return lax.ppermute(block, axis, route)]
    all_to_all x1 -> x0, starting transfers between devices: 4.14 us -> none  [shards(): lax.all_to_all(partial_value.reshape(groups, CAP, width), 'expert', split...]
    all_to_all x1 -> x0, waiting for transfers between devices: 3.14 us -> none  [shards(): lax.all_to_all(partial_value.reshape(groups, CAP, width), 'expert', split...]
  transfers between devices with their start and end apart: 2 -> 0, of which waited for: 2 -> 0; matrix products, arithmetic and copies ran while one was open for 18% -> 0% of each run, Pallas kernels for 0% -> 0%
where the time goes in v1:
time: 36.3 us; the launch traced here: 36 us
  Pallas kernels  28.3 us (78%)
  local copies, waits for them, and re-layouts  7.11 us (20%)
  between operations  0.65 us (2%)
    pallas_call x1, Pallas kernels, shards(): pl.pallas_call(functools.partial(exchange, sections, chips, flight), out_...  25.7 us
    unnamed x12, local copies, waits for them, and re-layouts  7.11 us
    pallas_call x1, Pallas kernels, shards(): pl.pallas_call(functools.partial(finish, flight), out_shape=(jax.ShapeDty...  2.55 us

profile of v1, /device:TPU:0, one launch (start us, length us, event | category | flops | bytes accessed | tf_op | source)
XLA Modules:
  0.0 36.0 jit_solution(6734767732847117392)
XLA Ops:
  0.6 0.0 copy-start
  0.6 1.9 %copy-done = bf16[1,1,4096,384]{3,2,1,0:T(8,128)(2,1)S(1)} copy-done((bf16[1,1,4096,384]{3,2,1,0:T(8,128)(2,1)S(1)}, bf16[1,1,4096,384]{3,2,1,0:T(8,128)(2,1)}, u32[]{:S(2)}) %copy-start) | copy-done | bytes 3145752
  2.5 0.0 copy-start.1
  2.5 1.4 %copy-done.1 = bf16[1,1,192,4096]{3,2,1,0:T(8,128)(2,1)S(1)} copy-done((bf16[1,1,192,4096]{3,2,1,0:T(8,128)(2,1)S(1)}, bf16[1,1,192,4096]{3,2,1,0:T(8,128)(2,1)}, u32[]{:S(2)}) %copy-start.1) | copy-done | bytes 1572888
  3.9 0.0 copy-start.2
  3.9 1.2 %copy-done.2 = bf16[1,128,4096]{2,1,0:T(8,128)(2,1)S(1)} copy-done((bf16[1,128,4096]{2,1,0:T(8,128)(2,1)S(1)}, bf16[1,128,4096]{2,1,0:T(8,128)(2,1)}, u32[]{:S(2)}) %copy-start.2) | copy-done | bytes 1048600
  5.2 0.0 copy-start.3
  5.2 1.2 %copy-done.3 = bf16[1,128,4096]{2,1,0:T(8,128)(2,1)S(1)} copy-done((bf16[1,128,4096]{2,1,0:T(8,128)(2,1)S(1)}, bf16[1,128,4096]{2,1,0:T(8,128)(2,1)}, u32[]{:S(2)}) %copy-start.3) | copy-done | bytes 1048600
  6.4 0.0 copy-start.4
  6.4 0.7 %copy-done.4 = s32[1,128,8]{1,2,0:T(8,128)S(1)} copy-done((s32[1,128,8]{1,2,0:T(8,128)S(1)}, s32[1,128,8]{1,2,0:T(8,128)}, u32[]{:S(2)}) %copy-start.4) | copy-done | bytes 4120
  7.1 0.0 copy-start.5
  7.1 0.7 %copy-done.5 = f32[1,128,8]{1,2,0:T(8,128)S(1)} copy-done((f32[1,128,8]{1,2,0:T(8,128)S(1)}, f32[1,128,8]{1,2,0:T(8,128)}, u32[]{:S(2)}) %copy-start.5) | copy-done | bytes 4120
  7.8 25.7 %shard_map.85 = (bf16[4096,384]{1,0:T(8,128)(2,1)S(1)}, bf16[192,4096]{1,0:T(8,128)(2,1)S(1)}, bf16[1,8,4096]{2,1,0:T(8,128)(2,1)S(1)}, f32[1,8,128]{2,1,0:T(8,128)S(1)}) custom-call(bf16[1,128,4096]{2,1,0:T(8,128)(2,1)S(1)} %copy-done.2, bf16[1,128,4096]{2,1,0:T(8,128)(2,1)S(1)} %copy-done.3, s32[1,8,128]{2,1,0:T(8,128)S(1)} %bitcast.2, ...), custom_call_target="tpu_custom_call" | custom-call | tf_op jit(solution)/shard_map/pallas_call | solution.py:270
  33.5 2.6 %shard_map.86 = (bf16[1,128,4096]{2,1,0:T(8,128)(2,1)}, bf16[1,1,4096,384]{3,2,1,0:T(8,128)(2,1)}, bf16[1,1,192,4096]{3,2,1,0:T(8,128)(2,1)}) custom-call(bf16[4096,384]{1,0:T(8,128)(2,1)S(1)} %get-tuple-element.7.ggu, bf16[192,4096]{1,0:T(8,128)(2,1)S(1)} %get-tuple-element.8.gdn, bf16[1,8,4096]{2,1,0:T(8,128)(2,1)S(1)} %get-tuple-element.9.sums, ...), custom_call_target="tpu_custom_call" | custom-call | tf_op jit(solution)/shard_map/pallas_call | solution.py:319
Async XLA Ops:
  0.6 1.9 %copy-start = (bf16[1,1,4096,384]{3,2,1,0:T(8,128)(2,1)S(1)}, bf16[1,1,4096,384]{3,2,1,0:T(8,128)(2,1)}, u32[]{:S(2)}) copy-start(bf16[1,1,4096,384]{3,2,1,0:T(8,128)(2,1)} %gu_hbm.1) | copy-start | bytes 9437188
  2.5 1.4 %copy-start.1 = (bf16[1,1,192,4096]{3,2,1,0:T(8,128)(2,1)S(1)}, bf16[1,1,192,4096]{3,2,1,0:T(8,128)(2,1)}, u32[]{:S(2)}) copy-start(bf16[1,1,192,4096]{3,2,1,0:T(8,128)(2,1)} %dn_hbm.1) | copy-start | bytes 4718596
  3.9 1.2 %copy-start.2 = (bf16[1,128,4096]{2,1,0:T(8,128)(2,1)S(1)}, bf16[1,128,4096]{2,1,0:T(8,128)(2,1)}, u32[]{:S(2)}) copy-start(bf16[1,128,4096]{2,1,0:T(8,128)(2,1)} %x_hbm.1) | copy-start | bytes 3145732
  5.2 1.2 %copy-start.3 = (bf16[1,128,4096]{2,1,0:T(8,128)(2,1)S(1)}, bf16[1,128,4096]{2,1,0:T(8,128)(2,1)}, u32[]{:S(2)}) copy-start(bf16[1,128,4096]{2,1,0:T(8,128)(2,1)} %u_hbm.1) | copy-start | bytes 3145732
  6.4 0.7 %copy-start.4 = (s32[1,128,8]{1,2,0:T(8,128)S(1)}, s32[1,128,8]{1,2,0:T(8,128)}, u32[]{:S(2)}) copy-start(s32[1,128,8]{1,2,0:T(8,128)} %param.8) | copy-start | bytes 12292
  7.1 0.7 %copy-start.5 = (f32[1,128,8]{1,2,0:T(8,128)S(1)}, f32[1,128,8]{1,2,0:T(8,128)}, u32[]{:S(2)}) copy-start(f32[1,128,8]{1,2,0:T(8,128)} %param.9) | copy-start | bytes 12292

commit v2 on v1

--- a/solution.py
+++ b/solution.py
@@ -192,17 +192,8 @@
 
     o_cols = width // OUT_PARTS
     pair = []
-    for k in range(OUT_PARTS):
-        cols = pl.ds(k * o_cols, o_cols)
-        part = dot(grad_both, w_gu[cols, :], ((1,), (1,))).astype(BF16)
-        keep[:, :, :, cols] = part.reshape(CORES, chips, CAP, o_cols)
-        copy = remote(
-            keep.at[1 - core, :, :, cols], pair_in.at[:, :, cols], p_send.at[k], p_recv.at[k], sibling
-        )
-        copy.start()
-        pair.append(copy)
-    sends.extend(pair)
-    for k in range(OUT_PARTS):
+
+    def pass_on(k):
         cols = pl.ds(k * o_cols, o_cols)
         pair[k].wait_recv()
         ro[:, :, cols] = (keep[core, :, :, cols].astype(F32) + pair_in[:, :, cols].astype(F32)).astype(BF16)
@@ -216,10 +207,28 @@
 
     for k in range(OUT_PARTS):
         cols = pl.ds(k * o_cols, o_cols)
+        part = dot(grad_both, w_gu[cols, :], ((1,), (1,))).astype(BF16)
+        keep[:, :, :, cols] = part.reshape(CORES, chips, CAP, o_cols)
+        copy = remote(
+            keep.at[1 - core, :, :, cols], pair_in.at[:, :, cols], p_send.at[k], p_recv.at[k], sibling
+        )
+        copy.start()
+        pair.append(copy)
+        if k > 0:
+            pass_on(k - 1)
+    sends.extend(pair)
+
+    def weights_part(k):
+        cols = pl.ds(k * o_cols, o_cols)
+        e_part = eg[:, :, :, cols].reshape(rows, o_cols)
+        gdn[:, cols] = dot(hidden, e_part, ((0,), (0,))).astype(BF16)
         x_part = xg[:, :, :, cols].reshape(rows, o_cols)
         ggu[cols, :] = dot(x_part, grad_both, ((0,), (0,))).astype(BF16)
-        e_part = eg[:, :, :, cols].reshape(rows, o_cols)
-        gdn[:, cols] = dot(hidden, e_part, ((0,), (0,))).astype(BF16)
+
+    weights_part(0)
+    pass_on(OUT_PARTS - 1)
+    for k in range(1, OUT_PARTS):
+        weights_part(k)
 
     per = chips // flight
     for k in range(OUT_PARTS):
@@ -264,7 +273,7 @@
     both_cols = gate_up.shape[3]
     hid = down.shape[2]
     dma = pltpu.SemaphoreType.DMA
-    anywhere = pl.BlockSpec(memory_space=pl.ANY)
+    hbm = pl.BlockSpec(memory_space=pltpu.HBM)
     vmem = pl.BlockSpec(memory_space=pltpu.VMEM)
     kept = pltpu.VMEM
     ggu, gdn, sums, sel = pl.pallas_call(
@@ -275,7 +284,7 @@
             kept((flight, CAP, width), BF16),
             kept((flight, CAP, tokens), F32),
         ),
-        in_specs=[anywhere] * 6,
+        in_specs=[hbm] * 6,
         out_specs=(vmem,) * 4,
         scratch_shapes=[
             pltpu.VMEM((tokens, width), BF16),
@@ -315,7 +324,10 @@
         compiler_params=pltpu.CompilerParams(
             collective_id=0, has_side_effects=True, vmem_limit_bytes=40 * 2**20
         ),
-    )(inputs, upstream, jnp.swapaxes(route, 1, 2), jnp.swapaxes(prob, 1, 2), gate_up, down)
+    )(*(
+        pltpu.with_memory_space_constraint(a, pltpu.HBM)
+        for a in (inputs, upstream, jnp.swapaxes(route, 1, 2), jnp.swapaxes(prob, 1, 2), gate_up, down)
+    ))
     return pl.pallas_call(
         functools.partial(finish, flight),
         out_shape=(
@@ -324,7 +336,7 @@
             jax.ShapeDtypeStruct(down.shape, BF16),
         ),
         in_specs=[vmem] * 4,
-        out_specs=(anywhere,) * 3,
+        out_specs=(hbm,) * 3,
         scratch_shapes=[pltpu.VMEM((tokens, width), BF16), dma((3,))],
         compiler_params=pltpu.CompilerParams(vmem_limit_bytes=16 * 2**20),
     )(ggu, gdn, sums, sel)

time: 36.3 us -> 28.3 us (0.78)
  local copies, waits for them, and re-layouts: 7.11 us -> 0 us
  Pallas kernels: 28.3 us -> 27.4 us
    unnamed x12 -> x0, local copies, waits for them, and re-layouts: 7.11 us -> none
    pallas_call x1, Pallas kernels: 25.7 us -> 24.9 us  [shards(): pl.pallas_call(functools.partial(exchange, sections, chips, flight), out_...]
where the time goes in v2:
time: 28.3 us; the launch traced here: 28.1 us
  Pallas kernels  27.4 us (97%)
  between operations  0.64 us (2%)
    pallas_call x1, Pallas kernels, shards(): pl.pallas_call(functools.partial(exchange, sections, chips, flight), out_...  24.9 us
    pallas_call x1, Pallas kernels, shards(): pl.pallas_call(functools.partial(finish, flight), out_shape=(jax.ShapeDty...  2.55 us

profile of v2, /device:TPU:0, one launch (start us, length us, event | category | flops | bytes accessed | tf_op | source)
XLA Modules:
  0.0 28.1 jit_solution(902366889412978326)
XLA Ops:
  0.6 24.9 %shard_map.85 = (bf16[4096,384]{1,0:T(8,128)(2,1)S(1)}, bf16[192,4096]{1,0:T(8,128)(2,1)S(1)}, bf16[1,8,4096]{2,1,0:T(8,128)(2,1)S(1)}, f32[1,8,128]{2,1,0:T(8,128)S(1)}) custom-call(bf16[1,128,4096]{2,1,0:T(8,128)(2,1)} %x_hbm.1, bf16[1,128,4096]{2,1,0:T(8,128)(2,1)} %u_hbm.1, s32[1,8,128]{2,1,0:T(8,128)} %bitcast.2, f32[1,8,128]{2,1,0:T(8,128)} %bitcast.3, ...), custom_call_target="tpu_custom_call" | custom-call | tf_op jit(solution)/shard_map/pallas_call | solution.py:279
  25.5 2.6 %shard_map.86 = (bf16[1,128,4096]{2,1,0:T(8,128)(2,1)}, bf16[1,1,4096,384]{3,2,1,0:T(8,128)(2,1)}, bf16[1,1,192,4096]{3,2,1,0:T(8,128)(2,1)}) custom-call(bf16[4096,384]{1,0:T(8,128)(2,1)S(1)} %get-tuple-element.7.ggu, bf16[192,4096]{1,0:T(8,128)(2,1)S(1)} %get-tuple-element.8.gdn, bf16[1,8,4096]{2,1,0:T(8,128)(2,1)S(1)} %get-tuple-element.9.sums, ...), custom_call_target="tpu_custom_call" | custom-call | tf_op jit(solution)/shard_map/pallas_call | solution.py:331

commit v3 on v2

--- a/solution.py
+++ b/solution.py
@@ -11,7 +11,8 @@
 CAP = 8
 CORES = 2
 E_PARTS = 2
-OUT_PARTS = 4
+OUT_PARTS = 2
+W_PARTS = 4
 MESH = pl.DeviceIdType.MESH
 F32 = jnp.float32
 BF16 = jnp.bfloat16
@@ -49,10 +50,11 @@
     hid = w_dn.shape[0]
 
     def chip_at(d):
-        return (chip + d) % chips
-
-    def chip_from(d):
-        return (chip + chips - d) % chips
+        at, bit = 0, 1
+        while bit < chips:
+            at = at + (chip // bit + d // bit) % 2 * bit
+            bit *= 2
+        return at
 
     def peer(d):
         return {"expert": chip_at(d) * CORES + core}
@@ -70,11 +72,13 @@
             )
         )
     ]
-    for load in loads:
-        load.start()
+    loads[0].start()
+    loads[1].start()
     barrier = pltpu.get_barrier_semaphore()
-    for target in [sibling, ahead, behind] + [peer(d) for d in range(1, chips)]:
+    for target in [ahead, behind, sibling] + [peer(d) for d in range(1, chips)]:
         pl.semaphore_signal(barrier, inc=1, device_id=target, device_id_type=MESH)
+    loads[2].start()
+    loads[3].start()
     loads[0].wait()
     loads[1].wait()
     before = (
@@ -100,18 +104,20 @@
     sends = [send_s]
 
     loads[2].wait()
+    loads[5].start()
+    loads[4].start()
     for e in range(flight):
         xb[e] = dot(picks[e], x_v[...], ((1,), (0,))).astype(BF16)
     for d in range(1, chips):
         copy = remote(
-            xb.at[chip_at(d) * CORES // SPLIT], xg.at[core, chip], x_send.at[d], x_recv.at[d], peer(d)
+            xb.at[chip_at(d) * CORES // SPLIT], xg.at[d, core], x_send.at[d], x_recv.at[d], peer(d)
         )
         copy.start()
         sends.append(copy)
-    copy = remote(xb.at[mine], xg.at[core, chip], xf_send.at[0], xf_recv.at[0], sibling)
+    copy = remote(xb.at[mine], xg.at[0, core], xf_send.at[0], xf_recv.at[0], sibling)
     copy.start()
     sends.append(copy)
-    xg[core, chip] = xb[mine]
+    xg[0, core] = xb[mine]
 
     loads[3].wait()
     send_s.wait_recv()
@@ -132,38 +138,47 @@
     sends.extend(z_copies)
 
     def relay(buf, d, cols, recv, f_send, f_recv):
-        slot = buf.at[core, chip_from(d), :, cols]
+        slot = buf.at[d, core, :, cols]
         remote(slot, slot, f_send, recv, sibling).wait_recv()
         copy = remote(slot, slot, f_send, f_recv, sibling)
         copy.start()
         sends.append(copy)
 
     def from_sibling(buf, d, cols, f_send, f_recv):
-        slot = buf.at[1 - core, chip_from(d), :, cols]
+        slot = buf.at[d, 1 - core, :, cols]
         remote(slot, slot, f_send, f_recv, sibling).wait_recv()
 
+    def send_e(k, d):
+        cols = pl.ds(k * e_cols, e_cols)
+        copy = remote(
+            er.at[chip_at(d) * CORES // SPLIT, :, cols],
+            eg.at[d, core, :, cols],
+            e_send.at[k, d],
+            e_recv.at[k, d],
+            peer(d),
+        )
+        copy.start()
+        sends.append(copy)
+
+    near = chips - chips // 4
+    groups = ((0, near), (near, chips))
     every = pl.ds(0, width)
     for d in range(1, chips):
         relay(xg, d, every, x_recv.at[d], xf_send.at[d], xf_recv.at[d])
     for k in range(E_PARTS):
         cols = pl.ds(k * e_cols, e_cols)
         z_copies[k].wait_recv()
-        for d in range(1, chips):
-            copy = remote(
-                er.at[chip_at(d) * CORES // SPLIT, :, cols],
-                eg.at[core, chip, :, cols],
-                e_send.at[k, d],
-                e_recv.at[k, d],
-                peer(d),
-            )
-            copy.start()
-            sends.append(copy)
+        for d in range(1, near):
+            send_e(k, d)
         copy = remote(
-            er.at[mine, :, cols], eg.at[core, chip, :, cols], ef_send.at[k, 0], ef_recv.at[k, 0], sibling
+            er.at[mine, :, cols], eg.at[0, core, :, cols], ef_send.at[k, 0], ef_recv.at[k, 0], sibling
         )
         copy.start()
         sends.append(copy)
-        eg[core, chip, :, cols] = er[mine, :, cols]
+        eg[0, core, :, cols] = er[mine, :, cols]
+    for k in range(E_PARTS):
+        for d in range(near, chips):
+            send_e(k, d)
     for d in range(chips):
         from_sibling(xg, d, every, xf_send.at[d], xf_recv.at[d])
     rows = CORES * chips * CAP
@@ -177,64 +192,89 @@
     slope = pre_up * sigma * (1.0 + pre_gate * (1.0 - sigma))
 
     loads[5].wait()
-    grad_hidden = None
-    for k in range(E_PARTS):
-        cols = pl.ds(k * e_cols, e_cols)
-        for d in range(1, chips):
-            relay(eg, d, cols, e_recv.at[k, d], ef_send.at[k, d], ef_recv.at[k, d])
-    for k in range(E_PARTS):
-        cols = pl.ds(k * e_cols, e_cols)
-        for d in range(chips):
-            from_sibling(eg, d, cols, ef_send.at[k, d], ef_recv.at[k, d])
-        term = dot(eg[:, :, :, cols].reshape(rows, e_cols), w_dn[:, cols], ((1,), (1,)))
-        grad_hidden = term if grad_hidden is None else grad_hidden + term
-    grad_both = jnp.concatenate([grad_hidden * slope, grad_hidden * silu_val], axis=1).astype(BF16)
-
     o_cols = width // OUT_PARTS
-    pair = []
-
-    def pass_on(k):
-        cols = pl.ds(k * o_cols, o_cols)
-        pair[k].wait_recv()
-        ro[:, :, cols] = (keep[core, :, :, cols].astype(F32) + pair_in[:, :, cols].astype(F32)).astype(BF16)
-        for d in range(1, chips):
+    pair = {}
+
+    def relay_group(g):
+        for k in range(E_PARTS):
+            cols = pl.ds(k * e_cols, e_cols)
+            for d in range(max(groups[g][0], 1), groups[g][1]):
+                relay(eg, d, cols, e_recv.at[k, d], ef_send.at[k, d], ef_recv.at[k, d])
+
+    def hidden_grads(g):
+        first, last = groups[g]
+        own = slice(first * CORES * CAP, last * CORES * CAP)
+        grad_hidden = None
+        for k in range(E_PARTS):
+            cols = pl.ds(k * e_cols, e_cols)
+            for d in range(first, last):
+                from_sibling(eg, d, cols, ef_send.at[k, d], ef_recv.at[k, d])
+            e_part = eg[first:last, :, :, cols].reshape((last - first) * CORES * CAP, e_cols)
+            term = dot(e_part, w_dn[:, cols], ((1,), (1,)))
+            grad_hidden = term if grad_hidden is None else grad_hidden + term
+        return jnp.concatenate([grad_hidden * slope[own], grad_hidden * silu_val[own]], axis=1).astype(BF16)
+
+    def to_pair(g, grads):
+        first, last = groups[g]
+        for k in range(OUT_PARTS):
+            cols = pl.ds(k * o_cols, o_cols)
+            part = dot(grads, w_gu[cols, :], ((1,), (1,))).astype(BF16)
+            keep[first:last, :, :, cols] = part.reshape(last - first, CORES, CAP, o_cols)
             copy = remote(
-                ro.at[chip_at(d), :, cols], rin.at[chip, :, cols], r_send.at[k, d], r_recv.at[k, d], peer(d)
+                keep.at[first:last, 1 - core, :, cols],
+                pair_in.at[first:last, :, cols],
+                p_send.at[g, k],
+                p_recv.at[g, k],
+                sibling,
             )
             copy.start()
+            pair[g, k] = copy
             sends.append(copy)
-        rin[chip, :, cols] = ro[chip, :, cols]
-
-    for k in range(OUT_PARTS):
-        cols = pl.ds(k * o_cols, o_cols)
-        part = dot(grad_both, w_gu[cols, :], ((1,), (1,))).astype(BF16)
-        keep[:, :, :, cols] = part.reshape(CORES, chips, CAP, o_cols)
-        copy = remote(
-            keep.at[1 - core, :, :, cols], pair_in.at[:, :, cols], p_send.at[k], p_recv.at[k], sibling
-        )
-        copy.start()
-        pair.append(copy)
-        if k > 0:
-            pass_on(k - 1)
-    sends.extend(pair)
+
+    def pass_on(g):
+        first, last = groups[g]
+        for k in range(OUT_PARTS):
+            cols = pl.ds(k * o_cols, o_cols)
+            pair[g, k].wait_recv()
+            ro[first:last, :, cols] = (
+                keep[first:last, core, :, cols].astype(F32) + pair_in[first:last, :, cols].astype(F32)
+            ).astype(BF16)
+            for d in range(max(first, 1), last):
+                copy = remote(
+                    ro.at[d, :, cols], rin.at[chip, :, cols], r_send.at[k, d], r_recv.at[k, d], peer(d)
+                )
+                copy.start()
+                sends.append(copy)
+            if first == 0:
+                rin[chip, :, cols] = ro[0, :, cols]
+
+    relay_group(0)
+    near_grads = hidden_grads(0)
+    to_pair(0, near_grads)
+    relay_group(1)
+    pass_on(0)
+    far_grads = hidden_grads(1)
+    to_pair(1, far_grads)
+    grad_both = jnp.concatenate([near_grads, far_grads], axis=0)
+    w_cols = width // W_PARTS
 
     def weights_part(k):
-        cols = pl.ds(k * o_cols, o_cols)
-        e_part = eg[:, :, :, cols].reshape(rows, o_cols)
+        cols = pl.ds(k * w_cols, w_cols)
+        e_part = eg[:, :, :, cols].reshape(rows, w_cols)
         gdn[:, cols] = dot(hidden, e_part, ((0,), (0,))).astype(BF16)
-        x_part = xg[:, :, :, cols].reshape(rows, o_cols)
+        x_part = xg[:, :, :, cols].reshape(rows, w_cols)
         ggu[cols, :] = dot(x_part, grad_both, ((0,), (0,))).astype(BF16)
 
     weights_part(0)
-    pass_on(OUT_PARTS - 1)
-    for k in range(1, OUT_PARTS):
+    pass_on(1)
+    for k in range(1, W_PARTS):
         weights_part(k)
 
     per = chips // flight
     for k in range(OUT_PARTS):
         cols = pl.ds(k * o_cols, o_cols)
         for d in range(1, chips):
-            slot = rin.at[chip_from(d), :, cols]
+            slot = rin.at[chip_at(d), :, cols]
             remote(slot, slot, r_send.at[k, d], r_recv.at[k, d], peer(d)).wait_recv()
         for e in range(flight):
             total = rin[e * per, :, cols].astype(F32)
@@ -296,12 +336,12 @@
             pltpu.VMEM((flight, CAP, tokens), F32),
             pltpu.VMEM((flight, CAP, tokens), F32),
             pltpu.VMEM((flight, CAP, width), BF16),
-            pltpu.VMEM((CORES, chips, CAP, width), BF16),
+            pltpu.VMEM((chips, CORES, CAP, width), BF16),
             pltpu.VMEM((flight, CAP, width), BF16),
             pltpu.VMEM((flight, CAP, width), BF16),
-            pltpu.VMEM((CORES, chips, CAP, width), BF16),
+            pltpu.VMEM((chips, CORES, CAP, width), BF16),
             pltpu.VMEM((chips, CAP, width), BF16),
-            pltpu.VMEM((CORES, chips, CAP, width), BF16),
+            pltpu.VMEM((chips, CORES, CAP, width), BF16),
             pltpu.VMEM((chips, CAP, width), BF16),
             pltpu.VMEM((chips, CAP, width), BF16),
             dma((6,)),
@@ -316,8 +356,8 @@
             dma((E_PARTS, chips)),
             dma((E_PARTS, chips)),
             dma((E_PARTS, chips)),
-            dma((OUT_PARTS,)),
-            dma((OUT_PARTS,)),
+            dma((2, OUT_PARTS)),
+            dma((2, OUT_PARTS)),
             dma((OUT_PARTS, chips)),
             dma((OUT_PARTS, chips)),
         ],

time: 28.3 us -> 30.2 us (1.067)
  Pallas kernels: 27.4 us -> 29.4 us
    pallas_call x1, Pallas kernels: 24.9 us -> 26.8 us  [shards(): pl.pallas_call(functools.partial(exchange, sections, chips, flight), out_...]
where the time goes in v3:
time: 30.2 us; the launch traced here: 30 us
  Pallas kernels  29.4 us (97%)
  between operations  0.64 us (2%)
    pallas_call x1, Pallas kernels, shards(): pl.pallas_call(functools.partial(exchange, sections, chips, flight), out_...  26.8 us
    pallas_call x1, Pallas kernels, shards(): pl.pallas_call(functools.partial(finish, flight), out_shape=(jax.ShapeDty...  2.55 us

profile of v3, /device:TPU:0, one launch (start us, length us, event | category | flops | bytes accessed | tf_op | source)
XLA Modules:
  0.0 30.0 jit_solution(15225761973833800790)
XLA Ops:
  0.6 26.8 %shard_map.85 = (bf16[4096,384]{1,0:T(8,128)(2,1)S(1)}, bf16[192,4096]{1,0:T(8,128)(2,1)S(1)}, bf16[1,8,4096]{2,1,0:T(8,128)(2,1)S(1)}, f32[1,8,128]{2,1,0:T(8,128)S(1)}) custom-call(bf16[1,128,4096]{2,1,0:T(8,128)(2,1)} %x_hbm.1, bf16[1,128,4096]{2,1,0:T(8,128)(2,1)} %u_hbm.1, s32[1,8,128]{2,1,0:T(8,128)} %bitcast.2, f32[1,8,128]{2,1,0:T(8,128)} %bitcast.3, ...), custom_call_target="tpu_custom_call" | custom-call | tf_op jit(solution)/shard_map/pallas_call | solution.py:319
  27.5 2.6 %shard_map.86 = (bf16[1,128,4096]{2,1,0:T(8,128)(2,1)}, bf16[1,1,4096,384]{3,2,1,0:T(8,128)(2,1)}, bf16[1,1,192,4096]{3,2,1,0:T(8,128)(2,1)}) custom-call(bf16[4096,384]{1,0:T(8,128)(2,1)S(1)} %get-tuple-element.7.ggu, bf16[192,4096]{1,0:T(8,128)(2,1)S(1)} %get-tuple-element.8.gdn, bf16[1,8,4096]{2,1,0:T(8,128)(2,1)S(1)} %get-tuple-element.9.sums, ...), custom_call_target="tpu_custom_call" | custom-call | tf_op jit(solution)/shard_map/pallas_call | solution.py:371

commit v4 on v3

--- a/solution.py
+++ b/solution.py
@@ -13,6 +13,8 @@
 E_PARTS = 2
 OUT_PARTS = 2
 W_PARTS = 4
+TURN_PARTS = 8
+GROUPS = 1
 MESH = pl.DeviceIdType.MESH
 F32 = jnp.float32
 BF16 = jnp.bfloat16
@@ -32,7 +34,7 @@
     sections, chips, flight,
     x_hbm, u_hbm, route_hbm, prob_hbm, gu_hbm, dn_hbm,
     ggu, gdn, sums, sel_out,
-    x_v, u_v, route_v, prob_v, w_gu, w_dn,
+    x_v, u_v, route_v, prob_v, w_gu, w_dn, w_gu_t, w_dn_t, x_t,
     s_out, s_in, xb, xg, eb, er, eg, pair_in, keep, ro, rin,
     local, s_sem, x_send, x_recv, xf_send, xf_recv,
     z_send, z_recv, e_send, e_recv, ef_send, ef_recv,
@@ -160,11 +162,20 @@
         copy.start()
         sends.append(copy)
 
-    near = chips - chips // 4
-    groups = ((0, near), (near, chips))
+    near = chips if GROUPS == 1 else chips - chips // 4
+    groups = ((0, near), (near, chips))[:GROUPS]
     every = pl.ds(0, width)
+    t_cols = width // TURN_PARTS
+    loads[5].wait()
+    for k in range(TURN_PARTS):
+        cols = pl.ds(k * t_cols, t_cols)
+        w_dn_t[cols, :] = w_dn[:, cols].T
     for d in range(1, chips):
         relay(xg, d, every, x_recv.at[d], xf_send.at[d], xf_recv.at[d])
+    loads[4].wait()
+    for k in range(TURN_PARTS // 2):
+        cols = pl.ds(k * t_cols, t_cols)
+        w_gu_t[:, cols] = w_gu[cols, :].T
     for k in range(E_PARTS):
         cols = pl.ds(k * e_cols, e_cols)
         z_copies[k].wait_recv()
@@ -182,7 +193,6 @@
     for d in range(chips):
         from_sibling(xg, d, every, xf_send.at[d], xf_recv.at[d])
     rows = CORES * chips * CAP
-    loads[4].wait()
     both = dot(xg[...].reshape(rows, width), w_gu[...], ((1,), (0,)))
     pre_gate = both[:, :hid]
     pre_up = both[:, hid:]
@@ -191,9 +201,14 @@
     hidden = (silu_val * pre_up).astype(BF16)
     slope = pre_up * sigma * (1.0 + pre_gate * (1.0 - sigma))
 
-    loads[5].wait()
     o_cols = width // OUT_PARTS
     pair = {}
+    for k in range(TURN_PARTS // 2, TURN_PARTS):
+        cols = pl.ds(k * t_cols, t_cols)
+        w_gu_t[:, cols] = w_gu[cols, :].T
+    for k in range(TURN_PARTS):
+        cols = pl.ds(k * t_cols, t_cols)
+        x_t[cols, :] = xg[:, :, :, cols].reshape(rows, t_cols).T
 
     def relay_group(g):
         for k in range(E_PARTS):
@@ -210,7 +225,7 @@
             for d in range(first, last):
                 from_sibling(eg, d, cols, ef_send.at[k, d], ef_recv.at[k, d])
             e_part = eg[first:last, :, :, cols].reshape((last - first) * CORES * CAP, e_cols)
-            term = dot(e_part, w_dn[:, cols], ((1,), (1,)))
+            term = dot(e_part, w_dn_t[cols, :], ((1,), (0,)))
             grad_hidden = term if grad_hidden is None else grad_hidden + term
         return jnp.concatenate([grad_hidden * slope[own], grad_hidden * silu_val[own]], axis=1).astype(BF16)
 
@@ -218,7 +233,7 @@
         first, last = groups[g]
         for k in range(OUT_PARTS):
             cols = pl.ds(k * o_cols, o_cols)
-            part = dot(grads, w_gu[cols, :], ((1,), (1,))).astype(BF16)
+            part = dot(grads, w_gu_t[:, cols], ((1,), (0,))).astype(BF16)
             keep[first:last, :, :, cols] = part.reshape(last - first, CORES, CAP, o_cols)
             copy = remote(
                 keep.at[first:last, 1 - core, :, cols],
@@ -248,25 +263,24 @@
             if first == 0:
                 rin[chip, :, cols] = ro[0, :, cols]
 
-    relay_group(0)
-    near_grads = hidden_grads(0)
-    to_pair(0, near_grads)
-    relay_group(1)
-    pass_on(0)
-    far_grads = hidden_grads(1)
-    to_pair(1, far_grads)
-    grad_both = jnp.concatenate([near_grads, far_grads], axis=0)
+    grads = []
+    for g in range(GROUPS):
+        relay_group(g)
+        if g > 0:
+            pass_on(g - 1)
+        grads.append(hidden_grads(g))
+        to_pair(g, grads[g])
+    grad_both = jnp.concatenate(grads, axis=0) if GROUPS > 1 else grads[0]
     w_cols = width // W_PARTS
 
     def weights_part(k):
         cols = pl.ds(k * w_cols, w_cols)
         e_part = eg[:, :, :, cols].reshape(rows, w_cols)
         gdn[:, cols] = dot(hidden, e_part, ((0,), (0,))).astype(BF16)
-        x_part = xg[:, :, :, cols].reshape(rows, w_cols)
-        ggu[cols, :] = dot(x_part, grad_both, ((0,), (0,))).astype(BF16)
+        ggu[cols, :] = dot(x_t[cols, :], grad_both, ((1,), (0,))).astype(BF16)
 
     weights_part(0)
-    pass_on(1)
+    pass_on(GROUPS - 1)
     for k in range(1, W_PARTS):
         weights_part(k)
 
@@ -333,6 +347,9 @@
             pltpu.VMEM((slots, tokens), F32),
             pltpu.VMEM((width, both_cols), BF16),
             pltpu.VMEM((hid, width), BF16),
+            pltpu.VMEM((both_cols, width), BF16),
+            pltpu.VMEM((width, hid), BF16),
+            pltpu.VMEM((width, groups * CAP), BF16),
             pltpu.VMEM((flight, CAP, tokens), F32),
             pltpu.VMEM((flight, CAP, tokens), F32),
             pltpu.VMEM((flight, CAP, width), BF16),
@@ -356,8 +373,8 @@
             dma((E_PARTS, chips)),
             dma((E_PARTS, chips)),
             dma((E_PARTS, chips)),
-            dma((2, OUT_PARTS)),
-            dma((2, OUT_PARTS)),
+            dma((GROUPS, OUT_PARTS)),
+            dma((GROUPS, OUT_PARTS)),
             dma((OUT_PARTS, chips)),
             dma((OUT_PARTS, chips)),
         ],

time: 30.2 us -> 28.5 us (0.944)
  Pallas kernels: 29.4 us -> 27.7 us
    pallas_call x1, Pallas kernels: 26.8 us -> 25.1 us  [shards(): pl.pallas_call(functools.partial(exchange, sections, chips, flight), out_...]
where the time goes in v4:
time: 28.5 us; the launch traced here: 28.3 us
  Pallas kernels  27.7 us (97%)
  between operations  0.64 us (2%)
    pallas_call x1, Pallas kernels, shards(): pl.pallas_call(functools.partial(exchange, sections, chips, flight), out_...  25.1 us
    pallas_call x1, Pallas kernels, shards(): pl.pallas_call(functools.partial(finish, flight), out_shape=(jax.ShapeDty...  2.55 us

profile of v4, /device:TPU:0, one launch (start us, length us, event | category | flops | bytes accessed | tf_op | source)
XLA Modules:
  0.0 28.3 jit_solution(3709392421725918989)
XLA Ops:
  0.6 25.1 %shard_map.85 = (bf16[4096,384]{1,0:T(8,128)(2,1)S(1)}, bf16[192,4096]{1,0:T(8,128)(2,1)S(1)}, bf16[1,8,4096]{2,1,0:T(8,128)(2,1)S(1)}, f32[1,8,128]{2,1,0:T(8,128)S(1)}) custom-call(bf16[1,128,4096]{2,1,0:T(8,128)(2,1)} %x_hbm.1, bf16[1,128,4096]{2,1,0:T(8,128)(2,1)} %u_hbm.1, s32[1,8,128]{2,1,0:T(8,128)} %bitcast.2, f32[1,8,128]{2,1,0:T(8,128)} %bitcast.3, ...), custom_call_target="tpu_custom_call" | custom-call | tf_op jit(solution)/shard_map/pallas_call | solution.py:333
  25.8 2.6 %shard_map.86 = (bf16[1,128,4096]{2,1,0:T(8,128)(2,1)}, bf16[1,1,4096,384]{3,2,1,0:T(8,128)(2,1)}, bf16[1,1,192,4096]{3,2,1,0:T(8,128)(2,1)}) custom-call(bf16[4096,384]{1,0:T(8,128)(2,1)S(1)} %get-tuple-element.7.ggu, bf16[192,4096]{1,0:T(8,128)(2,1)S(1)} %get-tuple-element.8.gdn, bf16[1,8,4096]{2,1,0:T(8,128)(2,1)S(1)} %get-tuple-element.9.sums, ...), custom_call_target="tpu_custom_call" | custom-call | tf_op jit(solution)/shard_map/pallas_call | solution.py:388

commit v5 on v3

--- a/solution.py
+++ b/solution.py
@@ -11,8 +11,9 @@
 CAP = 8
 CORES = 2
 E_PARTS = 2
-OUT_PARTS = 2
+OUT_PARTS = 4
 W_PARTS = 4
+TURN_PARTS = 4
 MESH = pl.DeviceIdType.MESH
 F32 = jnp.float32
 BF16 = jnp.bfloat16
@@ -32,7 +33,7 @@
     sections, chips, flight,
     x_hbm, u_hbm, route_hbm, prob_hbm, gu_hbm, dn_hbm,
     ggu, gdn, sums, sel_out,
-    x_v, u_v, route_v, prob_v, w_gu, w_dn,
+    x_v, u_v, route_v, prob_v, w_gu, w_dn, x_t,
     s_out, s_in, xb, xg, eb, er, eg, pair_in, keep, ro, rin,
     local, s_sem, x_send, x_recv, xf_send, xf_recv,
     z_send, z_recv, e_send, e_recv, ef_send, ef_recv,
@@ -75,7 +76,7 @@
     loads[0].start()
     loads[1].start()
     barrier = pltpu.get_barrier_semaphore()
-    for target in [ahead, behind, sibling] + [peer(d) for d in range(1, chips)]:
+    for target in [behind, sibling] + [peer(d) for d in range(1, chips)]:
         pl.semaphore_signal(barrier, inc=1, device_id=target, device_id_type=MESH)
     loads[2].start()
     loads[3].start()
@@ -97,7 +98,7 @@
         sel_out[e] = chosen
         s_out[e] = chosen * weight
         picks.append(chosen.astype(BF16))
-    pl.semaphore_wait(barrier, chips + 2)
+    pl.semaphore_wait(barrier, chips + 1)
 
     send_s = remote(s_out, s_in, s_sem.at[0], s_sem.at[1], ahead)
     send_s.start()
@@ -160,15 +161,15 @@
         copy.start()
         sends.append(copy)
 
-    near = chips - chips // 4
-    groups = ((0, near), (near, chips))
     every = pl.ds(0, width)
     for d in range(1, chips):
         relay(xg, d, every, x_recv.at[d], xf_send.at[d], xf_recv.at[d])
+    loads[4].wait()
+    loads[5].wait()
     for k in range(E_PARTS):
         cols = pl.ds(k * e_cols, e_cols)
         z_copies[k].wait_recv()
-        for d in range(1, near):
+        for d in range(1, chips):
             send_e(k, d)
         copy = remote(
             er.at[mine, :, cols], eg.at[0, core, :, cols], ef_send.at[k, 0], ef_recv.at[k, 0], sibling
@@ -176,13 +177,9 @@
         copy.start()
         sends.append(copy)
         eg[0, core, :, cols] = er[mine, :, cols]
-    for k in range(E_PARTS):
-        for d in range(near, chips):
-            send_e(k, d)
     for d in range(chips):
         from_sibling(xg, d, every, xf_send.at[d], xf_recv.at[d])
     rows = CORES * chips * CAP
-    loads[4].wait()
     both = dot(xg[...].reshape(rows, width), w_gu[...], ((1,), (0,)))
     pre_gate = both[:, :hid]
     pre_up = both[:, hid:]
@@ -191,82 +188,62 @@
     hidden = (silu_val * pre_up).astype(BF16)
     slope = pre_up * sigma * (1.0 + pre_gate * (1.0 - sigma))
 
-    loads[5].wait()
     o_cols = width // OUT_PARTS
     pair = {}
-
-    def relay_group(g):
-        for k in range(E_PARTS):
-            cols = pl.ds(k * e_cols, e_cols)
-            for d in range(max(groups[g][0], 1), groups[g][1]):
-                relay(eg, d, cols, e_recv.at[k, d], ef_send.at[k, d], ef_recv.at[k, d])
-
-    def hidden_grads(g):
-        first, last = groups[g]
-        own = slice(first * CORES * CAP, last * CORES * CAP)
-        grad_hidden = None
-        for k in range(E_PARTS):
-            cols = pl.ds(k * e_cols, e_cols)
-            for d in range(first, last):
-                from_sibling(eg, d, cols, ef_send.at[k, d], ef_recv.at[k, d])
-            e_part = eg[first:last, :, :, cols].reshape((last - first) * CORES * CAP, e_cols)
-            term = dot(e_part, w_dn[:, cols], ((1,), (1,)))
-            grad_hidden = term if grad_hidden is None else grad_hidden + term
-        return jnp.concatenate([grad_hidden * slope[own], grad_hidden * silu_val[own]], axis=1).astype(BF16)
-
-    def to_pair(g, grads):
-        first, last = groups[g]
-        for k in range(OUT_PARTS):
-            cols = pl.ds(k * o_cols, o_cols)
-            part = dot(grads, w_gu[cols, :], ((1,), (1,))).astype(BF16)
-            keep[first:last, :, :, cols] = part.reshape(last - first, CORES, CAP, o_cols)
+    t_cols = width // TURN_PARTS
+    for k in range(TURN_PARTS):
+        cols = pl.ds(k * t_cols, t_cols)
+        x_t[cols, :] = xg[:, :, :, cols].reshape(rows, t_cols).T
+
+    def to_pair(k):
+        cols = pl.ds(k * o_cols, o_cols)
+        part = dot(grad_both, w_gu[cols, :], ((1,), (1,))).astype(BF16)
+        keep[:, :, :, cols] = part.reshape(chips, CORES, CAP, o_cols)
+        copy = remote(
+            keep.at[:, 1 - core, :, cols], pair_in.at[:, :, cols], p_send.at[k], p_recv.at[k], sibling
+        )
+        copy.start()
+        pair[k] = copy
+        sends.append(copy)
+
+    def pass_on(k):
+        cols = pl.ds(k * o_cols, o_cols)
+        pair[k].wait_recv()
+        ro[:, :, cols] = (keep[:, core, :, cols].astype(F32) + pair_in[:, :, cols].astype(F32)).astype(BF16)
+        for d in range(1, chips):
             copy = remote(
-                keep.at[first:last, 1 - core, :, cols],
-                pair_in.at[first:last, :, cols],
-                p_send.at[g, k],
-                p_recv.at[g, k],
-                sibling,
+                ro.at[d, :, cols], rin.at[chip, :, cols], r_send.at[k, d], r_recv.at[k, d], peer(d)
             )
             copy.start()
-            pair[g, k] = copy
             sends.append(copy)
-
-    def pass_on(g):
-        first, last = groups[g]
-        for k in range(OUT_PARTS):
-            cols = pl.ds(k * o_cols, o_cols)
-            pair[g, k].wait_recv()
-            ro[first:last, :, cols] = (
-                keep[first:last, core, :, cols].astype(F32) + pair_in[first:last, :, cols].astype(F32)
-            ).astype(BF16)
-            for d in range(max(first, 1), last):
-                copy = remote(
-                    ro.at[d, :, cols], rin.at[chip, :, cols], r_send.at[k, d], r_recv.at[k, d], peer(d)
-                )
-                copy.start()
-                sends.append(copy)
-            if first == 0:
-                rin[chip, :, cols] = ro[0, :, cols]
-
-    relay_group(0)
-    near_grads = hidden_grads(0)
-    to_pair(0, near_grads)
-    relay_group(1)
-    pass_on(0)
-    far_grads = hidden_grads(1)
-    to_pair(1, far_grads)
-    grad_both = jnp.concatenate([near_grads, far_grads], axis=0)
+        rin[chip, :, cols] = ro[0, :, cols]
+
+    for k in range(E_PARTS):
+        cols = pl.ds(k * e_cols, e_cols)
+        for d in range(1, chips):
+            relay(eg, d, cols, e_recv.at[k, d], ef_send.at[k, d], ef_recv.at[k, d])
+    grad_hidden = None
+    for k in range(E_PARTS):
+        cols = pl.ds(k * e_cols, e_cols)
+        for d in range(chips):
+            from_sibling(eg, d, cols, ef_send.at[k, d], ef_recv.at[k, d])
+        term = dot(eg[:, :, :, cols].reshape(rows, e_cols), w_dn[:, cols], ((1,), (1,)))
+        grad_hidden = term if grad_hidden is None else grad_hidden + term
+    grad_both = jnp.concatenate([grad_hidden * slope, grad_hidden * silu_val], axis=1).astype(BF16)
+    for k in range(OUT_PARTS):
+        to_pair(k)
+        if k > 0:
+            pass_on(k - 1)
     w_cols = width // W_PARTS
 
     def weights_part(k):
         cols = pl.ds(k * w_cols, w_cols)
         e_part = eg[:, :, :, cols].reshape(rows, w_cols)
         gdn[:, cols] = dot(hidden, e_part, ((0,), (0,))).astype(BF16)
-        x_part = xg[:, :, :, cols].reshape(rows, w_cols)
-        ggu[cols, :] = dot(x_part, grad_both, ((0,), (0,))).astype(BF16)
+        ggu[cols, :] = dot(x_t[cols, :], grad_both, ((1,), (0,))).astype(BF16)
 
     weights_part(0)
-    pass_on(1)
+    pass_on(OUT_PARTS - 1)
     for k in range(1, W_PARTS):
         weights_part(k)
 
@@ -333,6 +310,7 @@
             pltpu.VMEM((slots, tokens), F32),
             pltpu.VMEM((width, both_cols), BF16),
             pltpu.VMEM((hid, width), BF16),
+            pltpu.VMEM((width, groups * CAP), BF16),
             pltpu.VMEM((flight, CAP, tokens), F32),
             pltpu.VMEM((flight, CAP, tokens), F32),
             pltpu.VMEM((flight, CAP, width), BF16),
@@ -356,8 +334,8 @@
             dma((E_PARTS, chips)),
             dma((E_PARTS, chips)),
             dma((E_PARTS, chips)),
-            dma((2, OUT_PARTS)),
-            dma((2, OUT_PARTS)),
+            dma((OUT_PARTS,)),
+            dma((OUT_PARTS,)),
             dma((OUT_PARTS, chips)),
             dma((OUT_PARTS, chips)),
         ],

time: 30.2 us -> 27.6 us (0.914)
  the two profiles are of different devices: /device:TPU:0 before, /device:TPU:25 now
where the time goes in v5:
time: 27.6 us; the launch traced here: 27.4 us
  Pallas kernels  26.8 us (97%)
  between operations  0.64 us (2%)
    pallas_call x1, Pallas kernels, shards(): pl.pallas_call(functools.partial(exchange, sections, chips, flight), out_...  24.2 us
    pallas_call x1, Pallas kernels, shards(): pl.pallas_call(functools.partial(finish, flight), out_shape=(jax.ShapeDty...  2.55 us

profile of v5, /device:TPU:25, one launch (start us, length us, event | category | flops | bytes accessed | tf_op | source)
XLA Modules:
  0.0 27.4 jit_solution(12739620442558024907)
XLA Ops:
  0.6 24.2 %shard_map.85 = (bf16[4096,384]{1,0:T(8,128)(2,1)S(1)}, bf16[192,4096]{1,0:T(8,128)(2,1)S(1)}, bf16[1,8,4096]{2,1,0:T(8,128)(2,1)S(1)}, f32[1,8,128]{2,1,0:T(8,128)S(1)}) custom-call(bf16[1,128,4096]{2,1,0:T(8,128)(2,1)} %x_hbm.1, bf16[1,128,4096]{2,1,0:T(8,128)(2,1)} %u_hbm.1, s32[1,8,128]{2,1,0:T(8,128)} %bitcast.2, f32[1,8,128]{2,1,0:T(8,128)} %bitcast.3, ...), custom_call_target="tpu_custom_call" | custom-call | tf_op jit(solution)/shard_map/pallas_call | solution.py:296
  24.9 2.6 %shard_map.86 = (bf16[1,128,4096]{2,1,0:T(8,128)(2,1)}, bf16[1,1,4096,384]{3,2,1,0:T(8,128)(2,1)}, bf16[1,1,192,4096]{3,2,1,0:T(8,128)(2,1)}) custom-call(bf16[4096,384]{1,0:T(8,128)(2,1)S(1)} %get-tuple-element.7.ggu, bf16[192,4096]{1,0:T(8,128)(2,1)S(1)} %get-tuple-element.8.gdn, bf16[1,8,4096]{2,1,0:T(8,128)(2,1)S(1)} %get-tuple-element.9.sums, ...), custom_call_target="tpu_custom_call" | custom-call | tf_op jit(solution)/shard_map/pallas_call | solution.py:349

commit v6 on v5

--- a/solution.py
+++ b/solution.py
@@ -32,8 +32,8 @@
 def exchange(
     sections, chips, flight,
     x_hbm, u_hbm, route_hbm, prob_hbm, gu_hbm, dn_hbm,
-    ggu, gdn, sums, sel_out,
-    x_v, u_v, route_v, prob_v, w_gu, w_dn, x_t,
+    ggu, gdn, sums, sel_out, x_t, grads,
+    x_v, u_v, route_v, prob_v, w_gu, w_dn,
     s_out, s_in, xb, xg, eb, er, eg, pair_in, keep, ro, rin,
     local, s_sem, x_send, x_recv, xf_send, xf_recv,
     z_send, z_recv, e_send, e_recv, ef_send, ef_recv,
@@ -230,6 +230,7 @@
         term = dot(eg[:, :, :, cols].reshape(rows, e_cols), w_dn[:, cols], ((1,), (1,)))
         grad_hidden = term if grad_hidden is None else grad_hidden + term
     grad_both = jnp.concatenate([grad_hidden * slope, grad_hidden * silu_val], axis=1).astype(BF16)
+    grads[...] = grad_both
     for k in range(OUT_PARTS):
         to_pair(k)
         if k > 0:
@@ -240,7 +241,8 @@
         cols = pl.ds(k * w_cols, w_cols)
         e_part = eg[:, :, :, cols].reshape(rows, w_cols)
         gdn[:, cols] = dot(hidden, e_part, ((0,), (0,))).astype(BF16)
-        ggu[cols, :] = dot(x_t[cols, :], grad_both, ((1,), (0,))).astype(BF16)
+        if k < W_PARTS // 2:
+            ggu[cols, :] = dot(x_t[cols, :], grad_both, ((1,), (0,))).astype(BF16)
 
     weights_part(0)
     pass_on(OUT_PARTS - 1)
@@ -262,21 +264,33 @@
         copy.wait_send()
 
 
-def finish(flight, ggu, gdn, sums, sel, gi_hbm, gu_hbm, dn_hbm, gi_v, sems):
-    copies = [
-        pltpu.make_async_copy(ggu, gu_hbm.at[0, 0], sems.at[0]),
-        pltpu.make_async_copy(gdn, dn_hbm.at[0, 0], sems.at[1]),
-    ]
+def finish(flight, ggu, gdn, sums, sel, x_t, grads, gi_hbm, gu_hbm, dn_hbm, gi_v, ggu_v, sems):
+    width = x_t.shape[0]
+    half = ggu.shape[0]
+    copies = []
+
+    def write(src, dst):
+        copy = pltpu.make_async_copy(src, dst, sems.at[len(copies)])
+        copy.start()
+        copies.append(copy)
+
+    write(ggu, gu_hbm.at[0, 0, pl.ds(0, half), :])
+    write(gdn, dn_hbm.at[0, 0])
+    step = width // W_PARTS
+    for k in range(W_PARTS // 2):
+        rows = pl.ds(k * step, step)
+        ahead = pl.ds(half + k * step, step)
+        ggu_v[rows, :] = dot(x_t[ahead, :], grads[...], ((1,), (0,))).astype(BF16)
+        write(ggu_v.at[rows, :], gu_hbm.at[0, 0, ahead, :])
+    for k in range(2):
+        cols = pl.ds(k * (width // 2), width // 2)
+        total = None
+        for e in range(flight):
+            term = dot(sel[e].astype(BF16), sums[e, :, cols], ((0,), (0,)))
+            total = term if total is None else total + term
+        gi_v[:, cols] = total.astype(BF16)
+        write(gi_v.at[:, cols], gi_hbm.at[0, :, cols])
     for copy in copies:
-        copy.start()
-    total = None
-    for e in range(flight):
-        term = dot(sel[e].astype(BF16), sums[e], ((0,), (0,)))
-        total = term if total is None else total + term
-    gi_v[...] = total.astype(BF16)
-    last = pltpu.make_async_copy(gi_v, gi_hbm.at[0], sems.at[2])
-    last.start()
-    for copy in copies + [last]:
         copy.wait()
 
 
@@ -293,16 +307,18 @@
     hbm = pl.BlockSpec(memory_space=pltpu.HBM)
     vmem = pl.BlockSpec(memory_space=pltpu.VMEM)
     kept = pltpu.VMEM
-    ggu, gdn, sums, sel = pl.pallas_call(
+    ggu, gdn, sums, sel, x_t, grads = pl.pallas_call(
         functools.partial(exchange, sections, chips, flight),
         out_shape=(
-            kept((width, both_cols), BF16),
+            kept((width // 2, both_cols), BF16),
             kept((hid, width), BF16),
             kept((flight, CAP, width), BF16),
             kept((flight, CAP, tokens), F32),
+            kept((width, groups * CAP), BF16),
+            kept((groups * CAP, both_cols), BF16),
         ),
         in_specs=[hbm] * 6,
-        out_specs=(vmem,) * 4,
+        out_specs=(vmem,) * 6,
         scratch_shapes=[
             pltpu.VMEM((tokens, width), BF16),
             pltpu.VMEM((tokens, width), BF16),
@@ -310,7 +326,6 @@
             pltpu.VMEM((slots, tokens), F32),
             pltpu.VMEM((width, both_cols), BF16),
             pltpu.VMEM((hid, width), BF16),
-            pltpu.VMEM((width, groups * CAP), BF16),
             pltpu.VMEM((flight, CAP, tokens), F32),
             pltpu.VMEM((flight, CAP, tokens), F32),
             pltpu.VMEM((flight, CAP, width), BF16),
@@ -353,11 +368,15 @@
             jax.ShapeDtypeStruct(gate_up.shape, BF16),
             jax.ShapeDtypeStruct(down.shape, BF16),
         ),
-        in_specs=[vmem] * 4,
+        in_specs=[vmem] * 6,
         out_specs=(hbm,) * 3,
-        scratch_shapes=[pltpu.VMEM((tokens, width), BF16), dma((3,))],
+        scratch_shapes=[
+            pltpu.VMEM((tokens, width), BF16),
+            pltpu.VMEM((width // 2, both_cols), BF16),
+            dma((4 + W_PARTS // 2,)),
+        ],
         compiler_params=pltpu.CompilerParams(vmem_limit_bytes=16 * 2**20),
-    )(ggu, gdn, sums, sel)
+    )(ggu, gdn, sums, sel, x_t, grads)
 
 
 def solution(mesh):

time: 27.6 us -> 27.6 us (level)
  no operation moved by 1% of the time
where the time goes in v6:
time: 27.6 us; the launch traced here: 27.4 us
  Pallas kernels  26.8 us (97%)
  between operations  0.64 us (2%)
    pallas_call x1, Pallas kernels, shards(): pl.pallas_call(functools.partial(exchange, sections, chips, flight), out_...  24.2 us
    pallas_call x1, Pallas kernels, shards(): pl.pallas_call(functools.partial(finish, flight), out_shape=(jax.ShapeDty...  2.56 us

profile of v6, /device:TPU:25, one launch (start us, length us, event | category | flops | bytes accessed | tf_op | source)
XLA Modules:
  0.0 27.4 jit_solution(18092595632103253306)
XLA Ops:
  0.6 24.2 %shard_map.85 = (bf16[2048,384]{1,0:T(8,128)(2,1)S(1)}, bf16[192,4096]{1,0:T(8,128)(2,1)S(1)}, bf16[1,8,4096]{2,1,0:T(8,128)(2,1)S(1)}, f32[1,8,128]{2,1,0:T(8,1...) custom-call(bf16[1,128,4096]{2,1,0:T(8,128)(2,1)} %x_hbm.1, bf16[1,128,4096]{2,1,0:T(8,128)(2,1)} %u_hbm.1, ...), custom_call_target="tpu_custom_call" | custom-call | tf_op jit(solution)/shard_map/pallas_call | solution.py:310
  24.9 2.6 %shard_map.86 = (bf16[1,128,4096]{2,1,0:T(8,128)(2,1)}, bf16[1,1,4096,384]{3,2,1,0:T(8,128)(2,1)}, bf16[1,1,192,4096]{3,2,1,0:T(8,128)(2,1)}) custom-call(bf16[2048,384]{1,0:T(8,128)(2,1)S(1)} %get-tuple-element.9.ggu, bf16[192,4096]{1,0:T(8,128)(2,1)S(1)} %get-tuple-element.10.gdn, bf16[1,8,4096]{2,1,0:T(8,128)(2,1)S(1)} %get-tuple-element.11.sums, ...), custom_call_target="tpu_custom_call" | custom-call | tf_op jit(solution)/shard_map/pallas_call | solution.py:364

commit v7 on v5

--- a/solution.py
+++ b/solution.py
@@ -10,7 +10,7 @@
 SPLIT = 8
 CAP = 8
 CORES = 2
-E_PARTS = 2
+E_PARTS = 4
 OUT_PARTS = 4
 W_PARTS = 4
 TURN_PARTS = 4
@@ -162,10 +162,6 @@
         sends.append(copy)
 
     every = pl.ds(0, width)
-    for d in range(1, chips):
-        relay(xg, d, every, x_recv.at[d], xf_send.at[d], xf_recv.at[d])
-    loads[4].wait()
-    loads[5].wait()
     for k in range(E_PARTS):
         cols = pl.ds(k * e_cols, e_cols)
         z_copies[k].wait_recv()
@@ -177,6 +173,10 @@
         copy.start()
         sends.append(copy)
         eg[0, core, :, cols] = er[mine, :, cols]
+    for d in range(1, chips):
+        relay(xg, d, every, x_recv.at[d], xf_send.at[d], xf_recv.at[d])
+    loads[4].wait()
+    loads[5].wait()
     for d in range(chips):
         from_sibling(xg, d, every, xf_send.at[d], xf_recv.at[d])
     rows = CORES * chips * CAP
@@ -218,17 +218,19 @@
             sends.append(copy)
         rin[chip, :, cols] = ro[0, :, cols]
 
-    for k in range(E_PARTS):
-        cols = pl.ds(k * e_cols, e_cols)
-        for d in range(1, chips):
-            relay(eg, d, cols, e_recv.at[k, d], ef_send.at[k, d], ef_recv.at[k, d])
     grad_hidden = None
-    for k in range(E_PARTS):
-        cols = pl.ds(k * e_cols, e_cols)
-        for d in range(chips):
-            from_sibling(eg, d, cols, ef_send.at[k, d], ef_recv.at[k, d])
-        term = dot(eg[:, :, :, cols].reshape(rows, e_cols), w_dn[:, cols], ((1,), (1,)))
-        grad_hidden = term if grad_hidden is None else grad_hidden + term
+    for step in range(E_PARTS + 2):
+        if step < E_PARTS:
+            cols = pl.ds(step * e_cols, e_cols)
+            for d in range(1, chips):
+                relay(eg, d, cols, e_recv.at[step, d], ef_send.at[step, d], ef_recv.at[step, d])
+        if step >= 2:
+            k = step - 2
+            cols = pl.ds(k * e_cols, e_cols)
+            for d in range(chips):
+                from_sibling(eg, d, cols, ef_send.at[k, d], ef_recv.at[k, d])
+            term = dot(eg[:, :, :, cols].reshape(rows, e_cols), w_dn[:, cols], ((1,), (1,)))
+            grad_hidden = term if grad_hidden is None else grad_hidden + term
     grad_both = jnp.concatenate([grad_hidden * slope, grad_hidden * silu_val], axis=1).astype(BF16)
     for k in range(OUT_PARTS):
         to_pair(k)

time: 27.6 us -> 27.1 us (0.982)
  the two profiles are of different devices: /device:TPU:25 before, /device:TPU:0 now
where the time goes in v7:
time: 27.1 us; the launch traced here: 26.9 us
  Pallas kernels  26.3 us (97%)
  between operations  0.64 us (2%)
    pallas_call x1, Pallas kernels, shards(): pl.pallas_call(functools.partial(exchange, sections, chips, flight), out_...  23.7 us
    pallas_call x1, Pallas kernels, shards(): pl.pallas_call(functools.partial(finish, flight), out_shape=(jax.ShapeDty...  2.55 us

profile of v7, /device:TPU:0, one launch (start us, length us, event | category | flops | bytes accessed | tf_op | source)
XLA Modules:
  0.0 26.9 jit_solution(14013450754002954645)
XLA Ops:
  0.6 23.7 %shard_map.85 = (bf16[4096,384]{1,0:T(8,128)(2,1)S(1)}, bf16[192,4096]{1,0:T(8,128)(2,1)S(1)}, bf16[1,8,4096]{2,1,0:T(8,128)(2,1)S(1)}, f32[1,8,128]{2,1,0:T(8,128)S(1)}) custom-call(bf16[1,128,4096]{2,1,0:T(8,128)(2,1)} %x_hbm.1, bf16[1,128,4096]{2,1,0:T(8,128)(2,1)} %u_hbm.1, s32[1,8,128]{2,1,0:T(8,128)} %bitcast.2, f32[1,8,128]{2,1,0:T(8,128)} %bitcast.3, ...), custom_call_target="tpu_custom_call" | custom-call | tf_op jit(solution)/shard_map/pallas_call | solution.py:298
  24.4 2.6 %shard_map.86 = (bf16[1,128,4096]{2,1,0:T(8,128)(2,1)}, bf16[1,1,4096,384]{3,2,1,0:T(8,128)(2,1)}, bf16[1,1,192,4096]{3,2,1,0:T(8,128)(2,1)}) custom-call(bf16[4096,384]{1,0:T(8,128)(2,1)S(1)} %get-tuple-element.7.ggu, bf16[192,4096]{1,0:T(8,128)(2,1)S(1)} %get-tuple-element.8.gdn, bf16[1,8,4096]{2,1,0:T(8,128)(2,1)S(1)} %get-tuple-element.9.sums, ...), custom_call_target="tpu_custom_call" | custom-call | tf_op jit(solution)/shard_map/pallas_call | solution.py:351

commit v8 on v7

--- a/solution.py
+++ b/solution.py
@@ -244,9 +244,8 @@
         gdn[:, cols] = dot(hidden, e_part, ((0,), (0,))).astype(BF16)
         ggu[cols, :] = dot(x_t[cols, :], grad_both, ((1,), (0,))).astype(BF16)
 
-    weights_part(0)
     pass_on(OUT_PARTS - 1)
-    for k in range(1, W_PARTS):
+    for k in range(W_PARTS):
         weights_part(k)
 
     per = chips // flight

time: 27.1 us -> 27.1 us (level)
  no operation moved by 1% of the time
where the time goes in v8:
time: 27.1 us; the launch traced here: 26.9 us
  Pallas kernels  26.3 us (97%)
  between operations  0.64 us (2%)
    pallas_call x1, Pallas kernels, shards(): pl.pallas_call(functools.partial(exchange, sections, chips, flight), out_...  23.7 us
    pallas_call x1, Pallas kernels, shards(): pl.pallas_call(functools.partial(finish, flight), out_shape=(jax.ShapeDty...  2.55 us

profile of v8, /device:TPU:0, one launch (start us, length us, event | category | flops | bytes accessed | tf_op | source)
XLA Modules:
  0.0 26.9 jit_solution(8021589219990339463)
XLA Ops:
  0.6 23.7 %shard_map.85 = (bf16[4096,384]{1,0:T(8,128)(2,1)S(1)}, bf16[192,4096]{1,0:T(8,128)(2,1)S(1)}, bf16[1,8,4096]{2,1,0:T(8,128)(2,1)S(1)}, f32[1,8,128]{2,1,0:T(8,128)S(1)}) custom-call(bf16[1,128,4096]{2,1,0:T(8,128)(2,1)} %x_hbm.1, bf16[1,128,4096]{2,1,0:T(8,128)(2,1)} %u_hbm.1, s32[1,8,128]{2,1,0:T(8,128)} %bitcast.2, f32[1,8,128]{2,1,0:T(8,128)} %bitcast.3, ...), custom_call_target="tpu_custom_call" | custom-call | tf_op jit(solution)/shard_map/pallas_call | solution.py:297
  24.4 2.6 %shard_map.86 = (bf16[1,128,4096]{2,1,0:T(8,128)(2,1)}, bf16[1,1,4096,384]{3,2,1,0:T(8,128)(2,1)}, bf16[1,1,192,4096]{3,2,1,0:T(8,128)(2,1)}) custom-call(bf16[4096,384]{1,0:T(8,128)(2,1)S(1)} %get-tuple-element.7.ggu, bf16[192,4096]{1,0:T(8,128)(2,1)S(1)} %get-tuple-element.8.gdn, bf16[1,8,4096]{2,1,0:T(8,128)(2,1)S(1)} %get-tuple-element.9.sums, ...), custom_call_target="tpu_custom_call" | custom-call | tf_op jit(solution)/shard_map/pallas_call | solution.py:350
